TPU v7x, 32 devices: a whole 2x2x4 slice. The times are simulated.
32 devices in a mesh: dp: 4 (over y, x), row: 2 (over core), col: 4 (over z).
Axes of the slice: x: 2, y: 2, z: 4, core: 2. Of those that a mesh axis runs over, the one named last changes fastest.
Arguments:
- tokens: bfloat16 [6144, 1536], P(('dp', 'row', 'col')), may hold values from -6 to 6
- cotangent: bfloat16 [6144, 1536], P(('dp', 'row', 'col')), may hold values from -6 to 6
- routes: int32 [6144, 8], P(('dp', 'row', 'col')), may hold values from 0 to 39, all different within a row; in each aligned block of 192 rows (0 to 191, 192 to 383, ...) at most 64 rows name the same one
- lengths: int32 [4, 4], P('dp'), may hold values from 1 to 1376, 1536 in all within a row
- gain_attn: bfloat16 [1536], replicated, may hold values from 0.5 to 1.5
- w_query: bfloat16 [1536, 1536], P(None, ('row', 'col')), may hold values from -0.21875 to 0.21875
- w_key: bfloat16 [1536, 512], P(None, ('row', 'col')), may hold values from -0.21875 to 0.21875
- w_value: bfloat16 [1536, 512], P(None, ('row', 'col')), may hold values from -0.15625 to 0.15625
- w_out: bfloat16 [1536, 1536], P(None, ('row', 'col')), may hold values from -0.875 to 0.875
- gain_moe: bfloat16 [1536], replicated, may hold values from 0.5 to 1.5
- w_router: bfloat16 [1536, 40], replicated, may hold values from -0.078125 to 0.078125
- w_gate: bfloat16 [40, 1536, 512], P(('row', 'col')), may hold values from -0.15625 to 0.15625
- w_up: bfloat16 [40, 1536, 512], P(('row', 'col')), may hold values from -0.15625 to 0.15625
- w_down: bfloat16 [40, 1536, 512], P(('row', 'col')), may hold values from -1 to 1
Outputs:
- mixed: bfloat16 [6144, 1536], P(('dp', 'row', 'col'))
- tokens_grad: float32 [6144, 1536], P(('dp', 'row', 'col'))
- gain_attn_grad: float32 [1536], replicated
- w_query_grad: float32 [1536, 1536], P('dp', ('row', 'col'))
- w_key_grad: float32 [1536, 512], P('dp', ('row', 'col'))
- w_value_grad: float32 [1536, 512], P('dp', ('row', 'col'))
- w_out_grad: float32 [1536, 1536], P('dp', ('row', 'col'))
- gain_moe_grad: float32 [1536], replicated
- w_router_grad: float32 [1536, 40], replicated
- w_gate_grad: float32 [40, 1536, 512], P(('row', 'col'), 'dp')
- w_up_grad: float32 [40, 1536, 512], P(('row', 'col'), 'dp')
- w_down_grad: float32 [40, 1536, 512], P(('row', 'col'), 'dp')
Inputs may be any that keep to these rules, and one draw needn't show every extreme that they name: `lengths`: each row sums to 1536 and holds one document of exactly 1376 tokens. `routes`: each token names 8 different experts; among the 192 rows of one device no expert is named by more than 64 rows, and in some device's rows one expert is named by exactly 64.
All inputs are finite; a program needn't handle non-finite values.
Results may differ from a plain program's by a relative error of at most 0.02.
The roundings to bfloat16 on the way count: a program that leaves them out, or rounds other values in their place, can miss the bound.
Values may be sent and summed in bfloat16 or wider, within the bound.
No kernel may reach another device: no remote copies, remote signals or barrier semaphores. Data moves between devices by JAX's collectives and lax.ppermute only.
A program may use at most 256 MiB of HBM per device.

v0:
```python
import math

import jax
import jax.numpy as jnp
import numpy as np
from jax import lax
from jax.experimental import pallas as pl
from jax.experimental.pallas import tpu as pltpu
from jax.sharding import PartitionSpec as P

HEAD_DIM = 64
EXPERTS = 40
TOP = 8
CAPACITY = 64
COLS = 4
LANES = 128
QUERY_BLOCK = 256
DOT_ROWS = 16

epsilon = 1e-06
rope_base = 10000.0
masked_score = -1e30
f32 = jnp.float32
bf16 = jnp.bfloat16
VMEM_LIMIT = 56 * 1024 * 1024

NT = (((1,), (1,)), ((), ()))
TN = (((0,), (0,)), ((), ()))


def dot(a, b):
    return jnp.dot(a, b, preferred_element_type=f32)


def dot_nt(a, b):
    return lax.dot_general(a, b, NT, preferred_element_type=f32)


def dot_tn(a, b):
    return lax.dot_general(a, b, TN, preferred_element_type=f32)


def lane_of(shape):
    return lax.broadcasted_iota(jnp.int32, shape, len(shape) - 1)


def call(
    kernel, grid, prefetch, in_specs, out_specs, out_shape, scratch=(), us=1.0, aliases=None
):
    return pl.pallas_call(
        kernel,
        grid_spec=pltpu.PrefetchScalarGridSpec(
            num_scalar_prefetch=prefetch,
            grid=grid,
            in_specs=in_specs,
            out_specs=out_specs,
            scratch_shapes=list(scratch),
        ),
        out_shape=out_shape,
        input_output_aliases=aliases or {},
        compiler_params=pltpu.CompilerParams(
            vmem_limit_bytes=VMEM_LIMIT, dimension_semantics=("arbitrary",) * len(grid)
        ),
        cost_estimate=pl.CostEstimate(
            flops=int(us * 1.1e9), bytes_accessed=int(us * 3.6e6), transcendentals=0
        ),
    )


def whole(shape):
    zeros = (0,) * len(shape)
    return pl.BlockSpec(shape, lambda *_: zeros)


def struct(shape, dtype):
    return jax.ShapeDtypeStruct(shape, dtype)


def turn_within_heads(values, sign):
    lane = lane_of(values.shape) % HEAD_DIM
    ahead = pltpu.roll(values, LANES - HEAD_DIM // 2, 1)
    behind = pltpu.roll(values, HEAD_DIM // 2, 1)
    return jnp.where(lane < HEAD_DIM // 2, -sign * ahead, sign * behind)


def project_kernel(
    tok_ref, gain_ref, w_ref, cos_ref, sin_ref, query_ref, key_ref, value_ref, normed_ref
):
    resid = tok_ref[...].astype(f32)
    inverse = lax.rsqrt(jnp.mean(resid * resid, axis=1, keepdims=True) + epsilon)
    normed = (resid * inverse * gain_ref[...]).astype(bf16)
    normed_ref[...] = normed
    raw = dot_nt(normed, w_ref[...])
    cosine, sine = cos_ref[...], sin_ref[...]

    def rot(values):
        return (values * cosine + turn_within_heads(values, 1.0) * sine).astype(bf16).astype(f32)

    first = rot(raw[:, :LANES])
    second = rot(raw[:, LANES : 2 * LANES])
    low = lane_of(first.shape) < HEAD_DIM
    scale = 1.0 / math.sqrt(HEAD_DIM)
    query_ref[0] = jnp.where(low, first * scale, 0.0).astype(bf16)
    query_ref[1] = jnp.where(low, 0.0, first * scale).astype(bf16)
    query_ref[2] = jnp.where(low, second * scale, 0.0).astype(bf16)
    key_ref[...] = jnp.where(low, pltpu.roll(second, HEAD_DIM, 1), second).astype(bf16)
    value_ref[...] = raw[:, 2 * LANES :].astype(bf16)


def project(tokens, gain, w_stack, cosine, sine):
    total, width = tokens.shape
    rows = 512
    lanes = pl.BlockSpec((rows, LANES), lambda j: (j, 0))
    wide = pl.BlockSpec((rows, width), lambda j: (j, 0))
    return call(
        project_kernel,
        (total // rows,),
        0,
        [wide, whole((1, width)), whole(w_stack.shape), lanes, lanes],
        [pl.BlockSpec((3, rows, LANES), lambda j: (0, j, 0)), lanes, lanes, wide],
        [
            struct((3, total, LANES), bf16),
            struct((total, LANES), bf16),
            struct((total, LANES), bf16),
            struct((total, width), bf16),
        ],
        us=0.5,
    )(tokens, gain, w_stack, cosine, sine)


def attend_kernel(query_ref, key_ref, value_ref, start_ref, packed_ref, plain_ref, total_ref, out_ref):
    blocks = query_ref.shape[1] // QUERY_BLOCK
    block = pl.program_id(0)
    for index in range(blocks):

        @pl.when(block == index)
        def _(index=index):
            rows = pl.ds(index * QUERY_BLOCK, QUERY_BLOCK)
            span = (index + 1) * QUERY_BLOCK
            row = index * QUERY_BLOCK + lax.broadcasted_iota(jnp.int32, (QUERY_BLOCK, span), 0)
            column = lane_of((QUERY_BLOCK, span))
            allowed = (column <= row) & (column >= start_ref[rows, :])

            def head(number, carry):
                scores = dot_nt(query_ref[number, rows, :], key_ref[0:span, :])
                scores = jnp.where(allowed, scores, masked_score)
                peak = jnp.max(scores, axis=1, keepdims=True)
                weights = jnp.exp(scores - peak)
                summed = jnp.sum(weights, axis=1, keepdims=True)
                probs = (weights * (1.0 / summed)).astype(bf16)
                out_ref[number] = dot(probs, value_ref[0:span, :])
                total = jnp.broadcast_to(peak + jnp.log(summed), (QUERY_BLOCK, LANES))
                total_ref[number, :, rows] = jnp.transpose(total)[0:8, :]
                return carry

            lax.fori_loop(0, 3, head, 0)
            low = lane_of((QUERY_BLOCK, LANES)) < HEAD_DIM
            one, two, three = out_ref[0], out_ref[1], out_ref[2]
            pair = jnp.where(low, one, two).astype(bf16)
            plain_ref[rows, 0:LANES] = pair
            plain_ref[rows, LANES : 2 * LANES] = jnp.where(low, three, 0.0).astype(bf16)
            if index < blocks // 2:
                packed_ref[rows, 0:LANES] = pair
                packed_ref[rows, LANES : 2 * LANES] = three.astype(bf16)
            else:
                back = pl.ds((index - blocks // 2) * QUERY_BLOCK, QUERY_BLOCK)
                before = packed_ref[back, LANES : 2 * LANES].astype(f32)
                packed_ref[back, LANES : 2 * LANES] = jnp.where(low, before, one).astype(bf16)
                packed_ref[back, 2 * LANES : 3 * LANES] = jnp.where(low, two, three).astype(bf16)


def attend(query, key, value, start):
    total = key.shape[0]
    return call(
        attend_kernel,
        (total // QUERY_BLOCK,),
        0,
        [whole(query.shape), whole(key.shape), whole(value.shape), whole(start.shape)],
        [whole((total // 2, 3 * LANES)), whole((total, 2 * LANES)), whole((3, 8, total))],
        [
            struct((total // 2, 3 * LANES), bf16),
            struct((total, 2 * LANES), bf16),
            struct((3, 8, total), f32),
        ],
        scratch=[pltpu.VMEM((3, QUERY_BLOCK, LANES), f32)],
        us=0.5,
    )(query, key, value, start)


def attend_back_kernel(
    query_ref, key_ref, value_ref, grad_ref, total_ref, start_ref, cos_ref, sin_ref, normed_ref, w_ref, gain_ref,
    blocks_ref, own_ref, out_ref, query_grad_ref, key_grad_ref, value_grad_ref, own_sum_ref
):
    blocks = query_ref.shape[1] // QUERY_BLOCK
    block = pl.program_id(0)
    scale = 1.0 / math.sqrt(HEAD_DIM)

    @pl.when(block == 0)
    def _():
        key_grad_ref[...] = jnp.zeros_like(key_grad_ref)
        value_grad_ref[...] = jnp.zeros_like(value_grad_ref)

    def back(values, cosine, sine):
        return values * cosine + turn_within_heads(values * sine, -1.0)

    for index in range(blocks):

        @pl.when(block == index)
        def _(index=index):
            rows = pl.ds(index * QUERY_BLOCK, QUERY_BLOCK)
            span = (index + 1) * QUERY_BLOCK
            row = index * QUERY_BLOCK + lane_of((span, QUERY_BLOCK))
            column = lax.broadcasted_iota(jnp.int32, (span, QUERY_BLOCK), 0)
            allowed = (column <= row) & (column >= start_ref[0:1, rows])
            low = lane_of((QUERY_BLOCK, LANES)) < HEAD_DIM

            def head(number, carry):
                query = query_ref[number, rows, :]
                tile = pl.multiple_of((number // 2) * LANES, LANES)
                upstream = grad_ref[rows, pl.ds(tile, LANES)].astype(f32)
                keep = low == (number != 1)
                upstream = jnp.where(keep, upstream, 0.0).astype(bf16)
                scores = dot_nt(key_ref[0:span, :], query)
                probs = jnp.exp(scores - total_ref[number, 0:1, rows])
                probs = jnp.where(allowed, probs, 0.0)
                prob_grad = dot_nt(value_ref[0:span, :], upstream)
                row_dot = jnp.sum(probs * prob_grad, axis=0, keepdims=True)
                score_grad = (probs * (prob_grad - row_dot)).astype(bf16)
                key_grad_ref[0:span, :] += dot(score_grad, query)
                value_grad_ref[0:span, :] += dot(probs.astype(bf16), upstream)
                query_grad_ref[number] = dot_tn(score_grad, key_ref[0:span, :]) * scale
                return carry

            lax.fori_loop(0, 3, head, 0)
            cosine, sine = cos_ref[rows, :], sin_ref[rows, :]
            pair = jnp.where(low, query_grad_ref[0], query_grad_ref[1])
            out_ref[rows, 0:LANES] = back(pair, cosine, sine).astype(bf16)
            out_ref[rows, LANES : 2 * LANES] = back(query_grad_ref[2], cosine, sine).astype(bf16)

    @pl.when(block == blocks - 1)
    def _():
        low = lane_of(key_grad_ref.shape) < HEAD_DIM
        key_grad = key_grad_ref[...]
        key_grad = key_grad + pltpu.roll(key_grad, HEAD_DIM, 1)
        key_grad = back(key_grad, cos_ref[...], sin_ref[...])
        before = out_ref[:, LANES : 2 * LANES].astype(f32)
        out_ref[:, LANES : 2 * LANES] = jnp.where(low, before, key_grad).astype(bf16)
        value_grad = value_grad_ref[...]
        value_grad = value_grad + pltpu.roll(value_grad, HEAD_DIM, 1)
        out_ref[:, 2 * LANES : 3 * LANES] = jnp.where(low, 0.0, value_grad).astype(bf16)
        chunk = 512
        own_sum_ref[...] = jnp.zeros_like(own_sum_ref)

        def add(index, carry):
            part = pl.ds(pl.multiple_of(index * chunk, chunk), chunk)
            own_sum_ref[...] += dot_tn(normed_ref[part, :], out_ref[part, :])
            return carry

        lax.fori_loop(0, out_ref.shape[0] // chunk, add, 0)
        own = own_sum_ref[...]
        own_ref[...] = own.astype(bf16)
        share = jnp.sum(own * w_ref[...].astype(f32), axis=1, keepdims=True) / gain_ref[...]
        share = jnp.transpose(jnp.broadcast_to(share, (share.shape[0], LANES)))[0:8, :]
        width = blocks_ref.shape[2]
        row = lax.broadcasted_iota(jnp.int32, (8, width), 0)
        terms = jnp.zeros((8, width), f32)
        for index in range(share.shape[1] // width):
            piece = share[:, index * width : (index + 1) * width]
            upper = piece.astype(bf16).astype(f32)
            terms = jnp.where(row == index, upper, jnp.where(row == index + 4, piece - upper, terms))
        terms = jnp.concatenate([terms, jnp.zeros((8, width), f32)], axis=0).astype(bf16)
        rows = blocks_ref.shape[1] - DOT_ROWS
        for index in range(blocks_ref.shape[0]):
            blocks_ref[index, 0:rows, :] = out_ref[index * rows : (index + 1) * rows, :]
            blocks_ref[index, rows:, :] = terms


def attend_back(query, key, value, grad, totals, start, cosine, sine, normed, w_natural, gain):
    total = key.shape[0]
    members = 2 * COLS
    rows = total // members + DOT_ROWS
    args = (query, key, value, grad, totals, start, cosine, sine, normed, w_natural, gain)
    return call(
        attend_back_kernel,
        (total // QUERY_BLOCK,),
        0,
        [whole(item.shape) for item in args],
        [whole((members, rows, 3 * LANES)), whole(w_natural.shape)],
        [struct((members, rows, 3 * LANES), bf16), struct(w_natural.shape, bf16)],
        scratch=[
            pltpu.VMEM((total, 3 * LANES), bf16),
            pltpu.VMEM((3, QUERY_BLOCK, LANES), f32),
            pltpu.VMEM((total, LANES), f32),
            pltpu.VMEM((total, LANES), f32),
            pltpu.VMEM(w_natural.shape, f32),
        ],
        us=0.5,
    )(*args)


def branch_operand(refs):
    rows = refs.shape[2]
    low = lane_of((rows, LANES)) < HEAD_DIM
    pairs, thirds = [], []
    for member in range(refs.shape[1]):
        one = refs[0, member, :, 0:LANES]
        mid = refs[0, member, :, LANES : 2 * LANES].astype(f32)
        end = refs[0, member, :, 2 * LANES : 3 * LANES].astype(f32)
        mid_turned = pltpu.roll(mid, HEAD_DIM, 1)
        end_turned = pltpu.roll(end, HEAD_DIM, 1)
        late = jnp.where(low, mid_turned, end_turned).astype(bf16)
        pairs.append(jnp.concatenate([one, late], axis=0))
        thirds.append((mid, end_turned))
    for member in range(0, refs.shape[1], 2):
        tops = []
        for which in range(2):
            left, right = thirds[member][which], thirds[member + 1][which]
            tops.append(jnp.where(low, left, pltpu.roll(right, HEAD_DIM, 1)).astype(bf16))
        pairs.append(jnp.concatenate(tops, axis=0))
    return jnp.concatenate(pairs, axis=1)


def branch_weights(ref):
    right = [ref[source, 0:LANES] for source in range(ref.shape[0])]
    return jnp.concatenate(right + [ref[source, LANES:] for source in range(ref.shape[0])], axis=0)


def hits_of(rank, local_experts):
    place = lax.broadcasted_iota(jnp.int32, (CAPACITY, rank.shape[1]), 0).astype(f32)
    return [place == rank[j : j + 1, :] for j in range(local_experts)]


def chosen_of(hits):
    return jnp.concatenate([jnp.where(hit, 1.0, 0.0).astype(bf16) for hit in hits], axis=0)


def middle_kernel(
    place_ref, att_mine_ref, att_other_ref, w_mine_ref, w_other_ref, tok_a_ref, tok_b_ref, routes_a_ref, routes_b_ref,
    gain_ref, w_router_ref, after_ref,
    x_ref, slot_gate_ref, rank_ref, gate_ref, normed_ref, middle_ref, gates_own_ref, gates_ref, ranks_ref
):
    step = pl.program_id(0)
    member = place_ref[2]
    cols = pl.num_programs(0)
    rows = tok_a_ref.shape[0]
    local_experts = x_ref.shape[0]
    branch = dot(branch_operand(att_mine_ref), branch_weights(w_mine_ref))
    branch = branch + dot(branch_operand(att_other_ref), branch_weights(w_other_ref))
    for half in range(2):
        tok_ref, routes_ref = ((tok_a_ref, routes_a_ref), (tok_b_ref, routes_b_ref))[half]
        middle = tok_ref[...].astype(f32) + branch[half * rows : (half + 1) * rows]
        inverse = lax.rsqrt(jnp.mean(middle * middle, axis=1, keepdims=True) + epsilon)
        normed = (middle * inverse * gain_ref[...]).astype(bf16)
        normed_ref[half, 0] = normed
        logits = dot_nt(w_router_ref[...], normed)
        padded = logits.shape[0]
        slot = lax.broadcasted_iota(jnp.int32, (padded, rows), 0)
        expert = (slot // 8) * local_experts + slot % 8
        expert = jnp.where(slot % 8 < local_experts, expert, -1).astype(f32)
        routes = routes_ref[0].astype(f32)
        named = expert == routes[0:1, 0:rows]
        for k in range(1, TOP):
            named = named | (expert == routes[k : k + 1, 0:rows])
        peak = jnp.max(jnp.where(named, logits, masked_score), axis=0, keepdims=True)
        weights = jnp.where(named, jnp.exp(logits - peak), 0.0)
        gates = weights / jnp.sum(weights, axis=0, keepdims=True)
        gates_ref[...] = gates
        ranks_ref[...] = jnp.where(named, dot(named.astype(f32).astype(bf16), after_ref[...]), -1.0)
        here = pl.ds(pl.multiple_of(member * 8, 8), 8)
        gate, rank = gates_ref[here, :], ranks_ref[here, :]
        rank_ref[half, 0] = rank
        gate_ref[half, 0] = gate
        hits = hits_of(rank, local_experts)
        slot_gate = jnp.concatenate(
            [jnp.sum(jnp.where(hit, gate[j : j + 1, :], 0.0), axis=1, keepdims=True) for j, hit in enumerate(hits)],
            axis=0,
        )
        chosen = chosen_of(hits)
        picked = dot(chosen, normed).astype(bf16)
        spread = jnp.broadcast_to(slot_gate, (slot_gate.shape[0], LANES))
        for j in range(local_experts):
            part = slice(j * CAPACITY, (j + 1) * CAPACITY)
            x_ref[j, half, 0] = picked[part]
            slot_gate_ref[j, half, 0] = spread[part]

        @pl.when(member == half * cols + step)
        def _(middle=middle, gates=gates):
            middle_ref[...] = middle
            gates_own_ref[...] = gates


def middle_and_dispatch(place, att, w_mine, w_other, tokens, routes, gain, w_router, local_experts):
    width = tokens.shape[1]
    half = COLS
    rows = tokens.shape[0] // (2 * half)
    padded = w_router.shape[0]
    after = jnp.asarray(np.triu(np.ones((rows, rows), np.float32), 1), bf16)
    slot_shape = (local_experts, 2, half, CAPACITY)
    early = pl.BlockSpec((rows, width), lambda i, p: (i, 0))
    late = pl.BlockSpec((rows, width), lambda i, p: (i + half, 0))
    routes_shape = (1,) + routes.shape[1:]
    return call(
        middle_kernel,
        (half,),
        1,
        [
            pl.BlockSpec((1, half, rows, 3 * LANES), lambda i, p: (p[0], 0, i, 0)),
            pl.BlockSpec((1, half, rows, 3 * LANES), lambda i, p: (1 - p[0], 0, i, 0)),
            whole(w_mine.shape),
            whole(w_other.shape),
            early,
            late,
            pl.BlockSpec(routes_shape, lambda i, p: (i, 0, 0)),
            pl.BlockSpec(routes_shape, lambda i, p: (i + half, 0, 0)),
            whole((1, width)),
            whole(w_router.shape),
            whole((rows, rows)),
        ],
        [
            pl.BlockSpec((local_experts, 2, 1, CAPACITY, width), lambda i, p: (0, 0, i, 0, 0)),
            pl.BlockSpec((local_experts, 2, 1, CAPACITY, LANES), lambda i, p: (0, 0, i, 0, 0)),
            pl.BlockSpec((2, 1, 8, rows), lambda i, p: (0, i, 0, 0)),
            pl.BlockSpec((2, 1, 8, rows), lambda i, p: (0, i, 0, 0)),
            pl.BlockSpec((2, 1, rows, width), lambda i, p: (0, i, 0, 0)),
            whole((rows, width)),
            whole((padded, rows)),
        ],
        [
            struct(slot_shape + (width,), bf16),
            struct(slot_shape + (LANES,), f32),
            struct((2, half, 8, rows), f32),
            struct((2, half, 8, rows), f32),
            struct((2, half, rows, width), bf16),
            struct((rows, width), f32),
            struct((padded, rows), f32),
        ],
        scratch=[pltpu.VMEM((padded, rows), f32), pltpu.VMEM((padded, rows), f32)],
        us=0.5,
    )(place, att, att, w_mine, w_other, tokens, tokens, routes, routes, gain, w_router, after)


def grad_dispatch_kernel(rank_ref, gate_ref, cot_ref, g_ref):
    local_experts = g_ref.shape[0]
    rows = cot_ref.shape[0] // 2
    for half in range(2):
        hits = hits_of(rank_ref[half], local_experts)
        gate = gate_ref[half]
        slot_gate = jnp.concatenate(
            [jnp.sum(jnp.where(hit, gate[j : j + 1, :], 0.0), axis=1, keepdims=True) for j, hit in enumerate(hits)],
            axis=0,
        )
        grads = (dot(chosen_of(hits), cot_ref[half * rows : (half + 1) * rows, :]) * slot_gate).astype(bf16)
        for j in range(local_experts):
            g_ref[j, half] = grads[j * CAPACITY : (j + 1) * CAPACITY]


def grad_dispatch(rank, gate, cotangents, local_experts):
    members, _, rows = rank.shape
    width = cotangents.shape[1]
    small = pl.BlockSpec((2, 8, rows), lambda j: (j, 0, 0))
    return call(
        grad_dispatch_kernel,
        (members // 2,),
        0,
        [small, small, pl.BlockSpec((2 * rows, width), lambda j: (j, 0))],
        pl.BlockSpec((local_experts, 2, CAPACITY, width), lambda j: (0, j, 0, 0)),
        struct((local_experts, members, CAPACITY, width), bf16),
        us=0.5,
    )(rank, gate, cotangents)


def expert_kernel(
    x_ref, gate_ref, w_gate_ref, w_up_ref, w_down_ref, forth_ref, active_ref, factor_ref, silu_ref
):
    gate_pre = dot(x_ref[0], w_gate_ref[0])
    up_pre = dot(x_ref[0], w_up_ref[0])
    sig = 1.0 / (1.0 + jnp.exp(-gate_pre))
    silu = gate_pre * sig
    silu_ref[0] = silu
    factor_ref[0] = up_pre * sig * (1.0 + gate_pre * (1.0 - sig))
    active_ref[0] = (silu * up_pre).astype(bf16)
    produced = dot_nt(active_ref[0], w_down_ref[0]).astype(bf16).astype(f32)
    forth_ref[0] = (produced * gate_ref[0, :, 0:1]).astype(bf16)


def run_experts(x, slot_gate, w_gate, w_up, w_down):
    count, slots, width = x.shape
    hidden = w_gate.shape[2]

    def per_expert(*shape):
        return pl.BlockSpec((1,) + shape, lambda e: (e, 0, 0))

    return call(
        expert_kernel,
        (count,),
        0,
        [per_expert(slots, width), per_expert(slots, LANES)] + [per_expert(width, hidden)] * 3,
        [per_expert(slots, width)] + [per_expert(slots, hidden)] * 3,
        [
            struct((count, slots, width), bf16),
            struct((count, slots, hidden), bf16),
            struct((count, slots, hidden), f32),
            struct((count, slots, hidden), f32),
        ],
        us=0.5,
    )(x, slot_gate, w_gate, w_up, w_down)


def expert_back_kernel(place_ref, *refs, fast):
    x_ref, g_ref, active_ref, factor_ref, silu_ref = refs[:5]
    w_gate_ref, w_up_ref, w_down_ref, back_ref, dots_ref = refs[5:10]
    grads, (gate_low_ref, up_low_ref) = refs[10:-2], refs[-2:]
    slots, width = g_ref.shape[1], g_ref.shape[2]
    chunk = 256
    active_grad = dot(g_ref[0], w_down_ref[0])
    gate_low_ref[...] = (active_grad * factor_ref[0]).astype(bf16)
    up_low_ref[...] = (active_grad * silu_ref[0]).astype(bf16)
    dots = jnp.sum(active_ref[0].astype(f32) * active_grad, axis=1, keepdims=True)
    dots_ref[0] = jnp.broadcast_to(dots, (slots, LANES))
    back_ref[0] = (dot_nt(gate_low_ref[...], w_gate_ref[0]) + dot_nt(up_low_ref[...], w_up_ref[0])).astype(bf16)

    def products(cols):
        x = x_ref[0, :, cols]
        yield 0, dot_tn(x, gate_low_ref[...]).astype(bf16)
        yield 1, dot_tn(x, up_low_ref[...]).astype(bf16)
        yield 2, dot_tn(g_ref[0, :, cols], active_ref[0]).astype(bf16)

    if fast:
        write_shards(place_ref, grads, products, width)
    else:

        def whole_columns(index, carry):
            cols = pl.ds(pl.multiple_of(index * chunk, chunk), chunk)
            for which, product in products(cols):
                grads[which][0, cols, :] = product
            return carry

        lax.fori_loop(0, width // chunk, whole_columns, 0)


def write_shards(place_ref, outs, products, width):
    send_a, keep_a, send_b, keep_b = outs
    x_bit, y_bit = place_ref[3], place_ref[4]
    shard = width // 4
    for dy in range(2):
        for dx in range(2):
            x, y = x_bit ^ dx, y_bit ^ dy
            cols = pl.ds(pl.multiple_of((y * 2 + x) * shard, shard), shard)
            for which, product in products(cols):
                side = product.shape[1] // 2
                (send_a if dx else keep_a)[0, which, y] = product[:, :side]
                (send_b if dy else keep_b)[0, which, x] = product[:, side:]


def run_experts_back(place, x, g, active, factor, silu, w_gate, w_up, w_down, first, count, fast):
    slots, width = g.shape[1], g.shape[2]
    hidden = w_gate.shape[2]

    def taken(*shape):
        return pl.BlockSpec((1,) + shape, lambda e, p: (e + first, 0, 0))

    def given(*shape):
        zeros = (0,) * len(shape)
        return pl.BlockSpec((1,) + shape, lambda e, p: (e,) + zeros)

    if fast:
        grad_shapes = [(3, 2, width // 4, hidden // 2)] * 4
    else:
        grad_shapes = [(width, hidden)] * 3
    return call(
        lambda *refs: expert_back_kernel(*refs, fast=fast),
        (count,),
        1,
        [taken(slots, width)] * 2 + [taken(slots, hidden)] * 3 + [taken(width, hidden)] * 3,
        [given(slots, width), given(slots, LANES)] + [given(*shape) for shape in grad_shapes],
        [struct((count, slots, width), bf16), struct((count, slots, LANES), f32)]
        + [struct((count,) + shape, bf16) for shape in grad_shapes],
        scratch=[pltpu.VMEM((slots, hidden), bf16)] * 2,
        us=0.5,
    )(place, x, g, active, factor, silu, w_gate, w_up, w_down)


DOT_LANES = 2 * LANES


def combine_kernel(place_ref, rank_ref, *refs, pieces, with_dots, mine):
    parts, rest = refs[:pieces], refs[pieces:]
    rows = rank_ref.shape[2]
    local_experts = sum(part.shape[0] for part in parts)
    hits = hits_of(rank_ref[0], local_experts)
    gathered = jnp.concatenate([part[j, 0] for part in parts for j in range(part.shape[0])], axis=0)
    summed = dot_tn(chosen_of(hits), gathered)
    out_ref = rest[-1]
    if mine:
        arrived_ref = rest[-2]
        summed = summed + arrived_ref[0, 0:rows, :].astype(f32)
    out_ref[0, 0:rows, :] = summed.astype(bf16)
    if with_dots:
        column = [part[j, 0][:, 0:1] for part in rest[:pieces] for j in range(part.shape[0])]
        scattered = [
            jnp.sum(jnp.where(hit, value, 0.0), axis=0, keepdims=True) for hit, value in zip(hits, column)
        ]
        scattered.append(jnp.zeros((DOT_ROWS - local_experts, rows), f32))
        scattered = jnp.concatenate(scattered, axis=0)
        upper = scattered.astype(bf16)
        out_ref[0, rows:, :] = jnp.zeros((DOT_ROWS, out_ref.shape[2]), bf16)
        out_ref[0, rows:, 0:rows] = upper
        out_ref[0, rows:, DOT_LANES : DOT_LANES + rows] = (scattered - upper.astype(f32)).astype(bf16)
        if mine:
            out_ref[0, rows:, 2 * DOT_LANES : 4 * DOT_LANES] = arrived_ref[0, rows:, 0 : 2 * DOT_LANES]


def combine(place, rank, parts, dots=None, arrived=None):
    mine = arrived is not None
    rows, width = rank.shape[2], parts[0].shape[-1]
    out_rows = rows + (DOT_ROWS if dots else 0)

    def member(step, p):
        return (p[0] if mine else 1 - p[0]) * COLS + step

    def slots_of(array):
        return pl.BlockSpec((array.shape[0], 1) + array.shape[2:], lambda j, p: (0, member(j, p), 0, 0))

    inputs = [
        part.reshape(part.shape[0], 2 * COLS, CAPACITY, part.shape[-1]) for part in list(parts) + list(dots or [])
    ]
    in_specs = [pl.BlockSpec((1, 8, rows), lambda j, p: (member(j, p), 0, 0))] + [slots_of(item) for item in inputs]
    by_chip = pl.BlockSpec((1, out_rows, width), lambda j, p: (j, 0, 0))
    if mine:
        inputs.append(arrived)
        in_specs.append(by_chip)
    return call(
        lambda *refs: combine_kernel(*refs, pieces=len(parts), with_dots=bool(dots), mine=mine),
        (COLS,),
        1,
        in_specs,
        by_chip,
        struct((COLS, out_rows, width), bf16),
        us=0.5,
    )(place, rank, *inputs)


def split_dot(dimension_numbers, values, exact):
    upper = values.astype(bf16)
    lower = (values - upper.astype(f32)).astype(bf16)
    return lax.dot_general(
        upper, exact, dimension_numbers, preferred_element_type=f32
    ) + lax.dot_general(lower, exact, dimension_numbers, preferred_element_type=f32)


EXTRA_SLOTS = 6


def middle_back_kernel(
    place_ref, sums_ref, gates_ref, middle_ref, cot_ref, gain_ref, w_router_ref, w_mine_ref, w_other_ref,
    grad_ref, branch_ref, attended_ref, extra_ref
):
    rows = middle_ref.shape[0]
    tail = sums_ref[:, rows : rows + 8, 0 : 4 * DOT_LANES].astype(f32)
    mine = tail[:, :, 0:rows] + tail[:, :, DOT_LANES : DOT_LANES + rows]
    other = tail[:, :, 2 * DOT_LANES : 2 * DOT_LANES + rows] + tail[:, :, 3 * DOT_LANES : 3 * DOT_LANES + rows]
    first_row = place_ref[0] == 0
    dots = jnp.concatenate([jnp.where(first_row, mine, other), jnp.where(first_row, other, mine)], axis=0)
    dots = dots.reshape(dots.shape[0] * 8, rows)
    gates = gates_ref[...]
    logit_grad = dots - gates * jnp.sum(dots, axis=0, keepdims=True)
    middle = middle_ref[...]
    inverse = lax.rsqrt(jnp.mean(middle * middle, axis=1, keepdims=True) + epsilon)
    unit = middle * inverse
    gain = gain_ref[...]
    grad = sums_ref[0, 0:rows].astype(f32)
    for index in range(1, sums_ref.shape[0]):
        grad = grad + sums_ref[index, 0:rows].astype(f32)
    grad = grad + split_dot(TN, logit_grad, w_router_ref[...])
    gain_grad = jnp.sum(grad * unit, axis=0, keepdims=True)
    scaled = grad * gain
    middle_grad = cot_ref[...].astype(f32) + inverse * (
        scaled - unit * jnp.mean(scaled * unit, axis=1, keepdims=True)
    )
    grad_ref[...] = middle_grad
    branch_grad = middle_grad.astype(bf16)
    branch_ref[0:rows, :] = branch_grad
    extra_ref[...] = jnp.zeros_like(extra_ref)
    for index in range(logit_grad.shape[0] // 8):
        first, lane = index // EXTRA_SLOTS * 8, index % EXTRA_SLOTS * DOT_LANES
        extra_ref[first : first + 8, lane : lane + rows] = logit_grad[index * 8 : index * 8 + 8]
    upper = gain_grad.astype(bf16).astype(f32)
    extra_ref[13:14, :] = upper
    extra_ref[14:15, :] = gain_grad - upper
    branch_ref[rows:, :] = extra_ref[...].astype(bf16)
    for which, ref in enumerate((w_mine_ref, w_other_ref)):
        line = place_ref[0] if which == 0 else 1 - place_ref[0]
        for col in range(ref.shape[0]):
            product = dot_nt(branch_grad, ref[col])
            member = line * COLS + col
            attended_ref[member, :, 0:LANES] = product[:, 0:LANES].astype(bf16)
            attended_ref[member, :, LANES : LANES + HEAD_DIM] = product[:, LANES:].astype(bf16)
            attended_ref[member, :, LANES + HEAD_DIM :] = jnp.zeros((product.shape[0], HEAD_DIM), bf16)


def middle_back(place, sums, gates, middle, cotangent, gain, w_router, w_mine, w_other):
    rows, width = middle.shape
    members = 2 * COLS
    args = (sums, gates, middle, cotangent, gain, w_router, w_mine, w_other)
    return call(
        middle_back_kernel,
        (1,),
        1,
        [whole(item.shape) for item in args],
        [whole((rows, width)), whole((rows + DOT_ROWS, width)), whole((members, rows, 2 * LANES))],
        [
            struct((rows, width), f32),
            struct((rows + DOT_ROWS, width), bf16),
            struct((members, rows, 2 * LANES), bf16),
        ],
        scratch=[pltpu.VMEM((DOT_ROWS, width), f32)],
        us=0.5,
    )(place, *args)


def input_grad_kernel(
    place_ref, grads_mine_ref, grads_other_ref, mine_a_ref, mine_b_ref, other_a_ref, other_b_ref,
    tok_ref, middle_grad_ref, gain_ref, out_ref, share_ref, sum_ref
):
    step = pl.program_id(0)
    first = place_ref[4] == 0

    def weights(a_ref, b_ref):
        a = jnp.concatenate([a_ref[index, 0] for index in range(a_ref.shape[0])], axis=0)
        b = jnp.concatenate([b_ref[index, 0] for index in range(b_ref.shape[0])], axis=0)
        upper, lower = jnp.where(first, a, b), jnp.where(first, b, a)
        return jnp.concatenate([upper, lower, lower[lower.shape[0] - HEAD_DIM :]], axis=0)

    rows = tok_ref.shape[0]
    part = dot(grads_mine_ref[0, 0:rows, :], weights(mine_a_ref, mine_b_ref))
    part = part + dot(grads_other_ref[0, 0:rows, :], weights(other_a_ref, other_b_ref))
    share = grads_mine_ref[0, rows:, :].astype(f32)[0:8] + grads_other_ref[0, rows:, :].astype(f32)[0:8]

    @pl.when(step == 0)
    def _():
        sum_ref[...] = part
        share_ref[...] = share

    @pl.when(step > 0)
    def _():
        sum_ref[...] += part
        share_ref[...] += share

    @pl.when(step == pl.num_programs(0) - 1)
    def _():
        resid = tok_ref[...].astype(f32)
        inverse = lax.rsqrt(jnp.mean(resid * resid, axis=1, keepdims=True) + epsilon)
        unit = resid * inverse
        scaled = sum_ref[...] * gain_ref[...]
        out_ref[...] = middle_grad_ref[...] + inverse * (
            scaled - unit * jnp.mean(scaled * unit, axis=1, keepdims=True)
        )


def input_grad(place, grads, weights, tokens, middle_grad, gain):
    rows, width = tokens.shape
    lanes = grads.shape[2]
    w_shape = (weights[0].shape[0], 1) + weights[0].shape[2:]
    return call(
        input_grad_kernel,
        (COLS,),
        1,
        [
            pl.BlockSpec((1, rows + DOT_ROWS, lanes), lambda c, p: (p[0] * COLS + c, 0, 0)),
            pl.BlockSpec((1, rows + DOT_ROWS, lanes), lambda c, p: ((1 - p[0]) * COLS + c, 0, 0)),
        ]
        + [pl.BlockSpec(w_shape, lambda c, p: (0, c, 0, 0))] * 4
        + [whole((rows, width)), whole((rows, width)), whole((1, width))],
        [whole((rows, width)), whole((8, lanes))],
        [struct((rows, width), f32), struct((8, lanes), f32)],
        scratch=[pltpu.VMEM((rows, width), f32)],
        us=0.5,
    )(place, grads, grads, *weights, tokens, middle_grad, gain)


def out_weights_kernel(place_ref, branch_ref, att_ref, normed_ref, own_ref, *refs, fast, local_experts):
    outs, small_ref, (sum_ref, gain_sum_ref) = refs[:-3], refs[-3], refs[-2:]
    step = pl.program_id(0)
    rows = att_ref.shape[0] // 2
    block = rows + DOT_ROWS

    @pl.when(step == 0)
    def _():
        sum_ref[...] = jnp.zeros_like(sum_ref)
        small_ref[...] = jnp.zeros_like(small_ref)
        gain_sum_ref[...] = jnp.zeros_like(gain_sum_ref)

    branch = jnp.concatenate([branch_ref[0:rows, :], branch_ref[block : block + rows, :]], axis=0)
    sum_ref[...] += dot_tn(branch, att_ref[...])
    for which in range(2):
        tail = branch_ref[which * block + rows : (which + 1) * block, :].astype(f32)
        slots = []
        for index in range(small_ref.shape[0] // 8):
            first, lane = index // EXTRA_SLOTS * 8, index % EXTRA_SLOTS * DOT_LANES
            slots.append(tail[first : first + 8, lane : lane + rows])
        logit_grad = jnp.concatenate(slots, axis=0)
        real = lax.broadcasted_iota(jnp.int32, logit_grad.shape, 0) % 8 < local_experts
        logit_grad = jnp.where(real, logit_grad, 0.0).astype(bf16)
        small_ref[...] += dot(logit_grad, normed_ref[which * rows : (which + 1) * rows, :])
        gain_sum_ref[...] += tail[8:16, :]

    @pl.when(step == pl.num_programs(0) - 1)
    def _():
        small_ref[7:8, :] = gain_sum_ref[5:6, :] + gain_sum_ref[6:7, :]

        def products(cols):
            own = own_ref[cols, 0 : 2 * LANES]
            out_one = sum_ref[cols, 0:LANES].astype(bf16)
            out_two = sum_ref[cols, LANES:]
            low = lane_of(out_two.shape) < HEAD_DIM
            tail = jnp.where(low, out_two, own_ref[cols, 2 * LANES :].astype(f32)).astype(bf16)
            yield 0, jnp.concatenate([own, out_one, tail], axis=1)

        if fast:
            write_shards(place_ref, outs, products, own_ref.shape[0])
        else:
            outs[0][...] = next(products(slice(0, own_ref.shape[0])))[1]


def out_weights(place, branch, attended, normed, own, padded, local_experts, fast):
    total, width = normed.shape
    rows = total // COLS
    blocks = branch.shape[0] // COLS
    if fast:
        shapes = [(1, 1, 2, width // 4, 2 * LANES)] * 4
    else:
        shapes = [(width, 4 * LANES)]
    return call(
        lambda *refs: out_weights_kernel(*refs, fast=fast, local_experts=local_experts),
        (COLS,),
        1,
        [
            pl.BlockSpec((blocks, width), lambda j, p: (j, 0)),
            pl.BlockSpec((rows, 2 * LANES), lambda j, p: (j, 0)),
            pl.BlockSpec((rows, width), lambda j, p: (j, 0)),
            whole(own.shape),
        ],
        [whole(shape) for shape in shapes] + [whole((padded, width))],
        [struct(shape, bf16) for shape in shapes] + [struct((padded, width), f32)],
        scratch=[pltpu.VMEM((width, 2 * LANES), f32), pltpu.VMEM((8, width), f32)],
        us=0.5,
    )(place, branch, attended, normed, own)


def first_sum_kernel(place_ref, keep_a_ref, got_a_ref, keep_b_ref, got_b_ref, *rest):
    send_a_ref, held_a_ref, send_b_ref, held_b_ref = rest[-4:]
    x_bit, y_bit = place_ref[3], place_ref[4]
    for bit, keep, got, send, held in (
        (y_bit, keep_a_ref, got_a_ref, send_a_ref, held_a_ref),
        (x_bit, keep_b_ref, got_b_ref, send_b_ref, held_b_ref),
    ):
        for kind in range(keep.shape[1]):
            held[0, kind] = (keep[0, kind, bit].astype(f32) + got[0, kind, bit].astype(f32)).astype(bf16)
            send[0, kind] = (keep[0, kind, 1 - bit].astype(f32) + got[0, kind, 1 - bit].astype(f32)).astype(bf16)


def first_sum(place, chunk, first=0, total=None, before=None):
    count, kinds, _, rows, cols = chunk[0].shape
    taken = pl.BlockSpec((1, kinds, 2, rows, cols), lambda e, p: (e, 0, 0, 0, 0))
    given = pl.BlockSpec((1, kinds, rows, cols), lambda e, p: (e + first, 0, 0, 0))
    extra = list(before) if before else []
    return call(
        first_sum_kernel,
        (count,),
        1,
        [taken] * 4 + [pl.BlockSpec(memory_space=pl.ANY)] * len(extra),
        [given] * 4,
        [struct((total or count, kinds, rows, cols), bf16)] * 4,
        us=0.5,
        aliases={5 + i: i for i in range(len(extra))},
    )(place, *chunk, *extra)


def last_sum_kernel(held_a_ref, got_a_ref, held_b_ref, got_b_ref, *rest):
    outs = rest[-3:]
    side = held_a_ref.shape[3]
    for which, out in enumerate(outs):
        out[0, :, :side] = held_a_ref[0, which].astype(f32) + got_a_ref[0, which].astype(f32)
        out[0, :, side:] = held_b_ref[0, which].astype(f32) + got_b_ref[0, which].astype(f32)


def last_sum(held_a, got_a, held_b, got_b, first, total, before):
    count, kinds, rows, cols = held_a.shape
    taken = pl.BlockSpec((1, kinds, rows, cols), lambda e: (e, 0, 0, 0))
    given = pl.BlockSpec((1, rows, 2 * cols), lambda e: (e + first, 0, 0))
    extra = list(before) if before else []
    return call(
        last_sum_kernel,
        (count,),
        0,
        [taken] * 4 + [pl.BlockSpec(memory_space=pl.ANY)] * len(extra),
        [given] * 3,
        [struct((total, rows, 2 * cols), f32)] * 3,
        us=0.5,
        aliases={4 + i: i for i in range(len(extra))},
    )(held_a, got_a, held_b, got_b, *extra)


def last_weights_kernel(held_a_ref, got_a_ref, held_b_ref, got_b_ref, query_ref, key_ref, value_ref, out_ref):
    left = jnp.transpose(held_a_ref[0, 0].astype(f32) + got_a_ref[0, 0].astype(f32))
    right = jnp.transpose(held_b_ref[0, 0].astype(f32) + got_b_ref[0, 0].astype(f32))
    cut = query_ref.shape[0]
    query_ref[...] = left[:cut]
    key_ref[...] = left[cut:]
    out_ref[...] = right[:cut]
    value_ref[...] = right[cut:]


def last_weights(parts, widths):
    rows = parts[0].shape[2]
    shapes = [(width, rows) for width in widths]
    return call(
        last_weights_kernel,
        (1,),
        0,
        [whole(part.shape) for part in parts],
        [whole(shape) for shape in shapes],
        [struct(shape, f32) for shape in shapes],
        us=0.5,
    )(*parts)


SWAP = [(0, 1), (1, 0)]


def after(value, *events):
    return lax.optimization_barrier((value,) + events)[0]


def gather_group(block):
    return lax.all_gather(block, ("row", "col"), axis=0, tiled=True)


def line_pieces(value):
    parts = [value]
    for distance in range(1, COLS):
        parts.insert(0, lax.ppermute(value, "col", [(i, (i + distance) % COLS) for i in range(COLS)]))
    return parts


def in_line_order(parts):
    parts = jnp.stack(parts + parts)
    return lax.dynamic_slice_in_dim(parts, COLS - 1 - lax.axis_index("col"), COLS, axis=0)


def flip(value, axis, bit, size):
    return lax.ppermute(value, axis, [(i, i ^ (1 << bit)) for i in range(size)])


def bits_of(size):
    return size.bit_length() - 1


def own_bit(axis, bit):
    return (lax.axis_index(axis) >> bit) & 1


def joined(mine, got, own):
    return jnp.where(own == 0, jnp.concatenate([mine, got]), jnp.concatenate([got, mine]))


def cube_step(value, axis, bit, size):
    return joined(value, flip(value, axis, bit, size), own_bit(axis, bit))


def lines_first(value):
    return jnp.transpose(value, (1, 0, 2, 3)).reshape(value.shape[1], value.shape[0] * value.shape[2], value.shape[3])


def cube_gather(value, axis, size):
    value = value[None]
    for bit in range(bits_of(size)):
        value = cube_step(value, axis, bit, size)
    return value


def sum_dp(value, sizes):
    for bit in range(bits_of(sizes["dp"])):
        value = value + flip(value, "dp", bit, sizes["dp"])
    return value


def reduce_over_dp(value, size):
    count = bits_of(size)
    value = value.reshape(value.shape[:1] + (2,) * count + value.shape[2:])
    current = value
    for bit in range(count - 1, -1, -1):
        own = own_bit("dp", bit)
        keep = lax.dynamic_index_in_dim(current, own, 1, keepdims=False)
        send = lax.dynamic_index_in_dim(current, 1 - own, 1, keepdims=False).astype(bf16)
        current = keep.astype(f32) + flip(send, "dp", bit, size).astype(f32)
    return current


def start_move(run, size):
    return flip(run[0], "dp", 0, size), flip(run[2], "dp", 1, size)


def second_move(sums, size):
    send_a, held_a, send_b, held_b = sums
    return held_a, flip(send_a, "dp", 1, size), held_b, flip(send_b, "dp", 0, size)


def layer(sizes):
    n_dp, n_row, n_col = sizes["dp"], sizes["row"], sizes["col"]
    members = n_row * n_col
    fast = n_dp == 4
    assert n_row == 2 and n_col == COLS and n_dp & (n_dp - 1) == 0

    def local(
        tokens, cotangent, routes, lengths, gain_attn, w_query, w_key, w_value, w_out,
        gain_moe, w_router, w_gate, w_up, w_down,
    ):
        rows, width = tokens.shape
        group = rows * members
        local_experts = w_gate.shape[0]
        row, col, dp = lax.axis_index("row"), lax.axis_index("col"), lax.axis_index("dp")
        place = jnp.stack([row, col, row * n_col + col, dp & 1, (dp >> 1) & 1]).astype(jnp.int32)
        gain_one = gain_attn.astype(f32)[None]
        gain_two = gain_moe.astype(f32)[None]

        tok_all = gather_group(tokens)
        w_in = jnp.concatenate([w_query.T, w_key.T, w_value.T], axis=0)
        out_share, in_share = rows // n_dp, w_in.shape[0] // n_dp
        shares = jnp.concatenate(
            [
                lax.dynamic_slice(w_out.T, (dp * out_share, 0), (out_share, width)),
                lax.dynamic_slice(w_in, (dp * in_share, 0), (in_share, width)),
                jnp.pad(routes.T.astype(bf16).reshape(1, TOP * rows), ((0, 7), (0, width - TOP * rows))),
            ],
            axis=0,
        )
        w_stack = jnp.concatenate([w_query.T, w_key.T, w_value.T, w_value.T], axis=0)
        w_natural = jnp.concatenate([w_query, w_key, w_value, w_value], axis=1)

        ends = jnp.cumsum(lengths[0])
        starts = ends - lengths[0]
        position = jnp.arange(group, dtype=jnp.int32)
        segment = jnp.sum((position[:, None] >= ends[None, :]).astype(jnp.int32), axis=1)
        member = segment[:, None] == jnp.arange(starts.shape[0], dtype=jnp.int32)[None, :]
        start = jnp.sum(jnp.where(member, starts[None, :], 0), axis=1).astype(jnp.int32)
        frequency = rope_base ** (-2.0 * jnp.arange(HEAD_DIM // 2, dtype=f32) / HEAD_DIM)
        angle = (position - start).astype(f32)[:, None] * frequency[None, :]
        cosine = jnp.tile(jnp.cos(angle), (1, 4))
        sine = jnp.tile(jnp.sin(angle), (1, 4))

        w_router_rows = w_router.T.reshape(members, local_experts, width)
        w_router_rows = jnp.pad(w_router_rows, ((0, 0), (0, 8 - local_experts), (0, 0)))
        w_router_rows = w_router_rows.reshape(members * 8, width)
        start_row = jnp.broadcast_to(start[None, :], (8, group))
        start = start[:, None]
        gain_column = gain_attn.astype(f32)[:, None]
        ready = (place, gain_one, gain_two, w_stack, w_natural, cosine, sine, w_router_rows, start, start_row, gain_column)
        shares, place, gain_one, gain_two, w_stack, w_natural, cosine, sine, w_router_rows, start, start_row, gain_column = (
            lax.optimization_barrier((shares,) + ready)
        )
        shares = line_pieces(after(shares, tok_all, cosine))

        query, key, value, normed_one = project(tok_all, gain_one, w_stack, cosine, sine)
        packed, attended, totals = attend(query, key, value, start)
        att_flat = gather_group(packed)
        att_all = att_flat.reshape((n_row, n_col) + packed.shape)
        shares = in_line_order(after(shares, packed))
        route_rows = shares[:, out_share + in_share]
        w_out_mine, in_part = shares[None, :, :out_share], shares[None, :, out_share : out_share + in_share]
        for bit in range(bits_of(n_dp)):
            w_out_mine = cube_step(w_out_mine, "dp", bit, n_dp)
        in_part = cube_step(in_part, "dp", 0, n_dp)
        w_out_mine = lines_first(w_out_mine)
        w_out_other = lax.ppermute(after(w_out_mine, in_part), "row", SWAP)
        route_rows = cube_gather(route_rows, "row", n_row)[:, :, : TOP * rows].reshape(members, TOP, rows)
        cot_all = gather_group(after(cotangent, w_out_other))
        x, slot_gate, rank, gate, normed_two, middle, gates = middle_and_dispatch(
            place, att_all, w_out_mine, w_out_other, tok_all, route_rows, gain_two, w_router_rows, local_experts
        )
        slots = members * CAPACITY
        x = x.reshape(local_experts, slots, width)
        slot_gate = slot_gate.reshape(local_experts, slots, LANES)
        rank, gate = rank.reshape(members, 8, rows), gate.reshape(members, 8, rows)
        forth, active, factor, silu = run_experts(x, slot_gate, w_gate, w_up, w_down)
        for bit in range(1, bits_of(n_dp) - 1):
            in_part = cube_step(in_part, "dp", bit, n_dp)
        last_bit = bits_of(n_dp) - 1
        in_got = after(flip(in_part, "dp", last_bit, n_dp), forth)
        forth_other = combine(place, after(rank, in_got), [forth])
        arrived = lax.ppermute(forth_other, "row", SWAP)
        g = grad_dispatch(after(rank, forth_other), gate, cot_all, local_experts)
        g = g.reshape(local_experts, slots, width)
        cuts = [0, 1, 3, local_experts]

        def backward(which, x):
            first, last = cuts[which], cuts[which + 1]
            return run_experts_back(place, x, g, active, factor, silu, w_gate, w_up, w_down, first, last - first, fast)

        runs = [backward(0, x)]
        forth_mine = combine(place, rank, [forth], arrived=after(arrived, runs[0][1]))
        forth_sums = lax.all_to_all(forth_mine, "col", 0, 0, tiled=True)
        runs.append(backward(1, after(x, forth_mine)))
        runs.append(backward(2, after(x, runs[1][1])))
        moved = [start_move(run[2:], n_dp) for run in runs] if fast else []
        back_parts, dot_parts = [run[0] for run in runs], [run[1] for run in runs]
        back_other = combine(place, after(rank, *moved[0]) if fast else rank, back_parts, dot_parts)
        arrived = lax.ppermute(back_other, "row", SWAP)
        back_mine = combine(place, rank, back_parts, dot_parts, arrived)
        back_mine = after(back_mine, forth_sums)
        back_sums = lax.all_to_all(back_mine, "col", 0, 0, tiled=True)

        if fast:
            w_in_parts = [in_part, in_got]
        else:
            own = own_bit("dp", last_bit)
            w_in_rows = lines_first(joined(in_part, in_got, own))[None]
            half = w_in_rows.shape[2] // 2
            upper, lower = w_in_rows[:, :, :half], w_in_rows[:, :, half:]
            w_in_parts = [jnp.where(place[4] == 0, upper, lower), jnp.where(place[4] == 0, lower, upper)]
        if fast:

            def chunk_of(which, *events):
                keep_a, keep_b = after((runs[which][3], runs[which][5]), *events)
                return keep_a, moved[which][0], keep_b, moved[which][1]

            sums = first_sum(place, chunk_of(0, back_mine), cuts[0], cuts[2])
            gate_middle = (sums[1],) + moved[1]
        else:
            gate_middle = ()
        w_in_parts += [lax.ppermute(after(part, back_mine), "row", SWAP) for part in w_in_parts]

        mixed = (middle + jnp.sum(after(forth_sums, back_mine).astype(f32), axis=0)).astype(bf16)

        middle_grad, branch_grad, attended_grad = middle_back(
            place, back_sums, gates, middle, cotangent, after(gain_two, mixed, *w_in_parts[2:], *gate_middle),
            w_router_rows, w_out_mine, w_out_other,
        )
        if fast:
            sums = first_sum(place, chunk_of(1, branch_grad), cuts[1], cuts[2], sums)
            started = [second_move(sums, n_dp)]
        attended_grad = lax.all_to_all(attended_grad, ("row", "col"), 0, 0, tiled=True)
        if fast:
            attended_grad = after(attended_grad, sums[1])
        branch_all = gather_group(branch_grad)

        attended_grad = attended_grad.reshape(group, 2 * LANES)
        projected_grad, own_grads = attend_back(
            query, key, value, attended_grad, totals, start_row, cosine, sine, normed_one, w_natural, gain_column
        )
        projected_all = lax.all_to_all(projected_grad, ("row", "col"), 0, 0, tiled=True)
        *w_parts, small = out_weights(
            place, branch_all, attended, normed_two.reshape(group, width), own_grads,
            members * 8, local_experts, fast,
        )
        arriving = ()
        if fast:
            w_moved = start_move(w_parts, n_dp)
            late = first_sum(place, chunk_of(2, small, started[0][1], started[0][3]))
            started.append(second_move(late, n_dp))
            w_first = first_sum(place, (w_parts[1], w_moved[0], w_parts[3], w_moved[1]))
            w_sums = second_move(w_first, n_dp)
            arriving = (w_first[1], started[1][0])
        else:
            cut = w_parts[0].reshape(1, n_dp, width // n_dp, w_parts[0].shape[1])
            w_sum = reduce_over_dp(cut, n_dp)[0]


        used = small.reshape(members, 8, width)[:, :local_experts].reshape(members * local_experts, width)
        both = sum_dp(jnp.concatenate([used, small[7:8]], axis=0), sizes)
        w_router_grad = both[: members * local_experts].T
        gain_moe_grad = both[members * local_experts]

        tokens_grad, share = input_grad(
            place, projected_all, w_in_parts, tokens, middle_grad, after(gain_one, w_parts[0], *arriving)
        )
        share = (share[0:4] + share[4:8]).reshape(8, width // 8)
        if fast:
            held_a, got_a, held_b, got_b = started[0]
            held_a, held_b = after((held_a, held_b), tokens_grad)
            expert_grads = last_sum(held_a, got_a, held_b, got_b, 0, local_experts, None)
            share = share + flip(share, "dp", 0, n_dp)
            held_a, got_a, held_b, got_b = started[1]
            held_a, held_b = after((held_a, held_b), share)
            expert_grads = last_sum(held_a, got_a, held_b, got_b, cuts[2], local_experts, expert_grads)
            gain_attn_grad = (share + flip(share, "dp", 1, n_dp)).reshape(width)
        else:
            gain_attn_grad = sum_dp(share, sizes).reshape(width)

        local_q, local_k = w_query.shape[1], w_key.shape[1]
        if fast:
            w_query_grad, w_key_grad, w_value_grad, w_out_grad = [
                item.T for item in last_weights(w_sums, (local_q, local_k, local_k, local_q))
            ]
        else:
            expert_grads = []
            for which in range(3):
                parts = [run[2 + which] for run in runs]
                parts = [part.reshape(part.shape[0], n_dp, width // n_dp, part.shape[2]) for part in parts]
                expert_grads.append(jnp.concatenate([reduce_over_dp(part, n_dp) for part in parts], axis=0))
            cut = local_q + local_k
            w_query_grad, w_key_grad = w_sum[:, :local_q], w_sum[:, local_q:cut]
            w_out_grad, w_value_grad = w_sum[:, cut : cut + local_q], w_sum[:, cut + local_q :]
        w_gate_grad, w_up_grad, w_down_grad = expert_grads
        return (
            mixed, tokens_grad, gain_attn_grad, w_query_grad, w_key_grad, w_value_grad, w_out_grad,
            gain_moe_grad, w_router_grad, w_gate_grad, w_up_grad, w_down_grad,
        )

    return local


def solution(mesh):
    return jax.shard_map(
        layer(dict(mesh.shape)),
        mesh=mesh,
        in_specs=(
            P(("dp", "row", "col"), None),
            P(("dp", "row", "col"), None),
            P(("dp", "row", "col"), None),
            P("dp", None),
            P(),
            P(None, ("row", "col")),
            P(None, ("row", "col")),
            P(None, ("row", "col")),
            P(None, ("row", "col")),
            P(),
            P(),
            P(("row", "col"), None, None),
            P(("row", "col"), None, None),
            P(("row", "col"), None, None),
        ),
        out_specs=(
            P(("dp", "row", "col"), None),
            P(("dp", "row", "col"), None),
            P(),
            P("dp", ("row", "col")),
            P("dp", ("row", "col")),
            P("dp", ("row", "col")),
            P("dp", ("row", "col")),
            P(),
            P(),
            P(("row", "col"), "dp", None),
            P(("row", "col"), "dp", None),
            P(("row", "col"), "dp", None),
        ),
        check_vma=False,
    )
```

profile of v0, /device:TPU:0, one launch (start us, length us, event | category | flops | bytes accessed | tf_op | source)
XLA Modules:
  0.0 544.5 jit_solution(1579451043684754870)
XLA Ops:
  21.8 42.3 %all-gather.5.cloned.1.call-done.tok_ref.tok_a_ref.tok_b_ref = bf16[1536,1536]{1,0:T(8,128)(2,1)} async-done(((bf16[192,1536]{1,0:T(8,128)(2,1)}), bf16[1536,1536]{1,0:T(8,128)(2,1)}) %all-gather.5.cloned.1.call-update) | async-done | bytes 4718608 | tf_op jit(solution)/shard_map/all_gather | solution.py:936
  71.0 8.9 %shard_map.238 = (bf16[3,1536,128]{2,1,0:T(8,128)(2,1)}, bf16[1536,128]{1,0:T(8,128)(2,1)}, bf16[1536,128]{1,0:T(8,128)(2,1)}, bf16[1536,1536]{1,0:T(8,128)(2,1)}) custom-call(bf16[1536,1536]{1,0:T(8,128)(2,1)} %all-gather.5.cloned.1.call-done.tok_ref.tok_a_ref.tok_b_ref, f32[1,1536]{1,0:T(1,128)} %broadcast_in_dim.46.gain_ref, ...), custom_call_target="tpu_custom_call" | custom-call | flops 550000000 | bytes 1800000 | tf_op jit(solution)/shard_map/pallas_call | solution.py:115
  79.8 18.5 %shard_map.239 = (bf16[768,384]{1,0:T(8,128)(2,1)}, bf16[1536,256]{1,0:T(8,128)(2,1)}, f32[3,8,1536]{2,1,0:T(8,128)}) custom-call(bf16[3,1536,128]{2,1,0:T(8,128)(2,1)} %get-tuple-element.134.query_ref, bf16[1536,128]{1,0:T(8,128)(2,1)} %get-tuple-element.135.key_ref, bf16[1536,128]{1,0:T(8,128)(2,1)} %get-tuple-element.136.value_ref, s32[1536,1]{1,0:T(8,128)} %copy.55.start_ref), custom_call_target="tpu_custom_call" | custom-call | flops 550000000 | bytes 1800000 | tf_op jit(solution)/shard_map/pallas_call | solution.py:174
  107.8 12.8 %collective-permute-done.3 = bf16[1,4,48,1536]{3,2,1,0:T(8,128)(2,1)S(1)} collective-permute-done((bf16[1,4,48,1536]{3,2,1,0:T(8,128)(2,1)S(1)}, bf16[1,4,48,1536]{3,2,1,0:T(8,128)(2,1)S(1)}, u32[]{:S(2)}, u32[]{:S(2)}) %collective-permute-start.3) | collective-permute-done | bytes 589856 | tf_op jit(solution)/shard_map/ppermute | solution.py:952
  122.4 17.9 %collective-permute-done.5 = bf16[1,4,80,1536]{3,2,1,0:T(8,128)(2,1)} collective-permute-done((bf16[1,4,80,1536]{3,2,1,0:T(8,128)(2,1)S(1)}, bf16[1,4,80,1536]{3,2,1,0:T(8,128)(2,1)}, u32[]{:S(2)}, u32[]{:S(2)}) %collective-permute-start.5) | collective-permute-done | bytes 983072 | tf_op jit(solution)/shard_map/ppermute | solution.py:952
  157.6 21.6 %shard_map.240 = (bf16[5,2,4,64,1536]{4,3,2,1,0:T(8,128)(2,1)}, f32[5,2,4,64,128]{4,3,2,1,0:T(8,128)}, f32[2,4,8,192]{3,2,1,0:T(8,128)}, f32[2,4,8,192]{3,2,1,0:...) custom-call(s32[5]{0:T(128)} %stack.42.place_ref.refs_0_, ...), custom_call_target="tpu_custom_call" | custom-call | flops 550000000 | bytes 1800000 | tf_op jit(solution)/shard_map/pallas_call | solution.py:402
  179.1 23.5 %shard_map.241 = (bf16[5,512,1536]{2,1,0:T(8,128)(2,1)}, bf16[5,512,512]{2,1,0:T(8,128)(2,1)}, f32[5,512,512]{2,1,0:T(8,128)}, f32[5,512,512]{2,1,0:T(8,128)}) custom-call(bf16[5,512,1536]{2,1,0:T(8,128)(2,1)} %bitcast.73, f32[5,512,128]{2,1,0:T(8,128)} %bitcast.109, bf16[5,1536,512]{2,1,0:T(8,128)(2,1)} %refs_6_.5, bf16[5,1536,512]{2,1,0:T(8,128)(2,1)} %refs_7_.5, ...), custom_call_target="tpu_custom_call" | custom-call | flops 550000000 | bytes 1800000 | tf_op jit(solution)/shard_map/pallas_call | solution.py:493
  208.6 7.3 %shard_map.243 = bf16[5,8,64,1536]{3,2,1,0:T(8,128)(2,1)} custom-call(f32[8,8,192]{2,1,0:T(8,128)} %bitcast.105, f32[8,8,192]{2,1,0:T(8,128)} %bitcast.114, bf16[1536,1536]{1,0:T(8,128)(2,1)} %all-gather.9.cloned.1.call-done.cot_ref), custom_call_target="tpu_custom_call" | custom-call | flops 550000000 | bytes 1800000 | tf_op jit(solution)/shard_map/pallas_call | solution.py:461
  215.8 11.4 %shard_map.244 = (bf16[1,512,1536]{2,1,0:T(8,128)(2,1)}, f32[1,512,128]{2,1,0:T(8,128)}, bf16[1,3,2,384,256]{4,3,2,1,0:T(8,128)(2,1)}, bf16[1,3,2,384,256]{4,3,2...) custom-call(s32[5]{0:T(128)} %stack.42.place_ref.refs_0_, ...), custom_call_target="tpu_custom_call" | custom-call | flops 550000000 | bytes 1800000 | tf_op jit(solution)/shard_map/pallas_call | solution.py:570
  230.6 6.3 %shard_map.245 = bf16[4,192,1536]{2,1,0:T(8,128)(2,1)} custom-call(s32[5]{0:T(128)} %stack.42.place_ref.refs_0_, f32[8,8,192]{2,1,0:T(8,128)} %bitcast.106, bf16[5,8,64,1536]{3,2,1,0:T(8,128)(2,1)} %bitcast.78, bf16[4,192,1536]{2,1,0:T(8,128)(2,1)} %copy-done.12), custom_call_target="tpu_custom_call" | custom-call | flops 550000000 | bytes 1800000 | tf_op jit(solution)/shard_map/pallas_call | solution.py:632
  236.9 14.3 %all-to-all-start = ((bf16[4,192,1536]{2,1,0:T(8,128)(2,1)}), bf16[4,192,1536]{2,1,0:T(8,128)(2,1)S(1)}, u32[]{:S(2)}, u32[]{:S(2)}) async-start(bf16[4,192,1536]{2,1,0:T(8,128)(2,1)} %shard_map.245), calls=%async_computation | async-start | bytes 4718592 | tf_op jit(solution)/shard_map/all_to_all | solution.py:1102
  251.2 17.2 %shard_map.246 = (bf16[2,512,1536]{2,1,0:T(8,128)(2,1)}, f32[2,512,128]{2,1,0:T(8,128)}, bf16[2,3,2,384,256]{4,3,2,1,0:T(8,128)(2,1)}, bf16[2,3,2,384,256]{4,3,2...) custom-call(s32[5]{0:T(128)} %stack.42.place_ref.refs_0_, ...), custom_call_target="tpu_custom_call" | custom-call | flops 550000000 | bytes 1800000 | tf_op jit(solution)/shard_map/pallas_call | solution.py:570
  268.4 17.2 %shard_map.247 = (bf16[2,512,1536]{2,1,0:T(8,128)(2,1)}, f32[2,512,128]{2,1,0:T(8,128)}, bf16[2,3,2,384,256]{4,3,2,1,0:T(8,128)(2,1)}, bf16[2,3,2,384,256]{4,3,2...) custom-call(s32[5]{0:T(128)} %stack.42.place_ref.refs_0_, ...), custom_call_target="tpu_custom_call" | custom-call | flops 550000000 | bytes 1800000 | tf_op jit(solution)/shard_map/pallas_call | solution.py:570
  298.1 6.7 %shard_map.249 = bf16[4,208,1536]{2,1,0:T(8,128)(2,1)} custom-call(s32[5]{0:T(128)} %stack.42.place_ref.refs_0_, f32[8,8,192]{2,1,0:T(8,128)} %bitcast.108, bf16[1,8,64,1536]{3,2,1,0:T(8,128)(2,1)} %bitcast.89, bf16[2,8,64,1536]{3,2,1,0:T(8,128)(2,1)} %bitcast.85, bf16[2,8,64,1536]{3,2,1,0:T(8,128)(2,1)} %bitcast.87, f32[1,8,64,128]{3,2,1,0:T(8,128)} %bitcast.111, ...), custom_call_target="tpu_custom_call" | custom-call | flops 550000000 | bytes 1800000 | tf_op jit(solution)/shard_map/pallas_call | solution.py:632
  321.5 43.1 %collective-permute-done.15.got_a_ref = bf16[2,3,2,384,256]{4,3,2,1,0:T(8,128)(2,1)S(1)} collective-permute-done((bf16[2,3,2,384,256]{4,3,2,1,0:T(8,128)(2,1)}, bf16[2,3,2,384,256]{4,3,2,1,0:T(8,128)(2,1)S(1)}, u32[]{:S(2)}, u32[]{:S(2)}) %collective-permute-start.15) | collective-permute-done | bytes 2359328 | tf_op jit(solution)/shard_map/ppermute | solution.py:952
  371.1 7.6 %shard_map.251 = (f32[192,1536]{1,0:T(8,128)}, bf16[208,1536]{1,0:T(8,128)(2,1)}, bf16[8,192,256]{2,1,0:T(8,128)(2,1)}) custom-call(s32[5]{0:T(128)} %stack.42.place_ref.refs_0_, bf16[4,208,1536]{2,1,0:T(8,128)(2,1)} %copy-done.4, f32[64,192]{1,0:T(8,128)} %get-tuple-element.175.gates_ref, f32[192,1536]{1,0:T(8,128)} %get-tuple-element.148.middle_ref, ...), custom_call_target="tpu_custom_call" | custom-call | flops 550000000 | bytes 1800000 | tf_op jit(solution)/shard_map/pallas_call | solution.py:705
  385.0 6.4 %shard_map.252 = (bf16[3,3,384,256]{3,2,1,0:T(8,128)(2,1)}, bf16[3,3,384,256]{3,2,1,0:T(8,128)(2,1)}, bf16[3,3,384,256]{3,2,1,0:T(8,128)(2,1)}, bf16[3,3,384,256]{3,2,1,0:T(8,128)(2,1)}) custom-call(s32[5]{0:T(128)} %stack.42.place_ref.refs_0_, ...), custom_call_target="tpu_custom_call", output_to_operand_aliasing={{0}: (5, {}), {1}: (6, {}), {2}: (7, {}), {3}: (8, {})} | custom-call | flops 550000000 | bytes 1800000 | tf_op jit(solution)/shard_map/pallas_call | solution.py:867
  395.0 21.8 %all-to-all-done.2 = bf16[8,192,256]{2,1,0:T(8,128)(2,1)S(1)} async-done(((bf16[8,192,256]{2,1,0:T(8,128)(2,1)}), bf16[8,192,256]{2,1,0:T(8,128)(2,1)S(1)}, u32[]{:S(2)}, u32[]{:S(2)}) %all-to-all-start.2) | async-done | bytes 786464 | tf_op jit(solution)/shard_map/all_to_all | solution.py:1142
  417.7 31.4 %shard_map.253 = (bf16[8,208,384]{2,1,0:T(8,128)(2,1)}, bf16[1536,384]{1,0:T(8,128)(2,1)}) custom-call(bf16[3,1536,128]{2,1,0:T(8,128)(2,1)} %get-tuple-element.134.query_ref, bf16[1536,128]{1,0:T(8,128)(2,1)} %get-tuple-element.135.key_ref, bf16[1536,128]{1,0:T(8,128)(2,1)} %get-tuple-element.136.value_ref, bf16[1536,256]{1,0:T(8,128)(2,1)} %bitcast.95, ...), custom_call_target="tpu_custom_call" | custom-call | flops 550000000 | bytes 1800000 | tf_op jit(solution)/shard_map/pallas_call | solution.py:283
  449.0 10.8 %all-to-all-start.3 = ((bf16[8,208,384]{2,1,0:T(8,128)(2,1)}), bf16[8,208,384]{2,1,0:T(8,128)(2,1)S(1)}, u32[]{:S(2)}, u32[]{:S(2)}) async-start(bf16[8,208,384]{2,1,0:T(8,128)(2,1)} %get-tuple-element.202), calls=%async_computation.3 | async-start | bytes 2555904 | tf_op jit(solution)/shard_map/all_to_all | solution.py:1151
  459.8 8.7 %shard_map.254 = (bf16[1,1,2,384,256]{4,3,2,1,0:T(8,128)(2,1)}, bf16[1,1,2,384,256]{4,3,2,1,0:T(8,128)(2,1)}, bf16[1,1,2,384,256]{4,3,2,1,0:T(8,128)(2,1)}, bf16...) custom-call(s32[5]{0:T(128)} %stack.42.place_ref.refs_0_, bf16[1664,1536]{1,0:T(8,128)(2,1)} %all-gather.11.cloned.1.call-done.refs_1_, ...), custom_call_target="tpu_custom_call" | custom-call | flops 550000000 | bytes 1800000 | tf_op jit(solution)/shard_map/pallas_call | solution.py:833
  494.5 9.0 %shard_map.257 = (f32[192,1536]{1,0:T(8,128)}, f32[8,384]{1,0:T(8,128)}) custom-call(s32[5]{0:T(128)} %stack.42.place_ref.refs_0_, bf16[8,208,384]{2,1,0:T(8,128)(2,1)} %copy-done.3, bf16[8,208,384]{2,1,0:T(8,128)(2,1)} %copy-done.3, bf16[2,4,80,1536]{3,2,1,0:T(8,128)(2,1)} %maximum_select_fusion.1.mine_a_ref, ...), custom_call_target="tpu_custom_call" | custom-call | flops 550000000 | bytes 1800000 | tf_op jit(solution)/shard_map/pallas_call | solution.py:764
  506.7 7.9 %collective-permute-done.23 = f32[8,192]{1,0:T(8,128)S(1)} collective-permute-done((f32[8,192]{1,0:T(8,128)S(1)}, f32[8,192]{1,0:T(8,128)S(1)}, u32[]{:S(2)}, u32[]{:S(2)}) %collective-permute-start.23) | collective-permute-done | bytes 6176 | tf_op jit(solution)/shard_map/ppermute | solution.py:952
  516.4 6.8 %shard_map.259 = (f32[5,384,512]{2,1,0:T(8,128)}, f32[5,384,512]{2,1,0:T(8,128)}, f32[5,384,512]{2,1,0:T(8,128)}) custom-call(bf16[3,3,384,256]{3,2,1,0:T(8,128)(2,1)} %get-tuple-element.238.held_a_ref, bf16[3,3,384,256]{3,2,1,0:T(8,128)(2,1)} %collective-permute-done.19.got_a_ref, bf16[3,3,384,256]{3,2,1,0:T(8,128)(2,1)} %get-tuple-element.239.held_b_ref, ...), custom_call_target="tpu_custom_call" | custom-call | flops 550000000 | bytes 1800000 | tf_op jit(solution)/shard_map/pallas_call | solution.py:892
  (194 shorter events, 150.5 us)
Async XLA Ops:
  7.2 56.9 %all-gather.5.cloned.1.call-start = ((), (), s32[]{:S(2)}) async-start(), calls=%async_computation.4 | async-start | bytes 5308416 | tf_op jit(solution)/shard_map/all_gather | solution.py:936
  8.0 149.6 %all-gather.7.cloned.1.call-start = ((), (), s32[]{:S(2)}) async-start(), calls=%async_computation.5 | async-start | bytes 5308416 | tf_op jit(solution)/shard_map/all_gather | solution.py:936
  65.0 37.3 %collective-permute-start.1 = (bf16[136,1536]{1,0:T(8,128)(2,1)S(1)}, bf16[136,1536]{1,0:T(8,128)(2,1)S(1)}, u32[]{:S(2)}, u32[]{:S(2)}) collective-permute-start(bf16[136,1536]{1,0:T(8,128)(2,1)S(1)} %fusion.2), channel_id=1, source_target_pairs={{0,2},{1,3},{2,0},{3,1},{4,6},{5,7},{6,4},{7,5},{8,10},{9,11},{10,... | collective-permute-start | bytes 1253384 | tf_op jit(solution)/shard_map/ppermute | solution.py:942
  65.5 36.7 %collective-permute-start.2 = (bf16[136,1536]{1,0:T(8,128)(2,1)S(1)}, bf16[136,1536]{1,0:T(8,128)(2,1)S(1)}, u32[]{:S(2)}, u32[]{:S(2)}) collective-permute-start(bf16[136,1536]{1,0:T(8,128)(2,1)S(1)} %fusion.2), channel_id=1, source_target_pairs={{0,1},{1,2},{2,3},{3,0},{4,5},{5,6},{6,7},{7,4},{8,9},{9,10},{10,1... | collective-permute-start | bytes 1253384 | tf_op jit(solution)/shard_map/ppermute | solution.py:942
  98.4 110.2 %all-gather.9.cloned.1.call-start = ((), (), s32[]{:S(2)}) async-start(), calls=%async_computation.6 | async-start | bytes 5308416 | tf_op jit(solution)/shard_map/all_gather | solution.py:936
  153.1 49.5 %collective-permute-start.8 = (bf16[2,4,80,1536]{3,2,1,0:T(8,128)(2,1)}, bf16[2,4,80,1536]{3,2,1,0:T(8,128)(2,1)}, u32[]{:S(2)}, u32[]{:S(2)}) collective-permute-start(bf16[2,4,80,1536]{3,2,1,0:T(8,128)(2,1)} %maximum_select_fusion.1.mine_a_ref), channel_id=1, source_target_pairs={{0,16},{8,24},{16,0},{24,8},{1,17},{9,25},{17,1},{25,9},{2,18},{10... | collective-permute-start | bytes 5898248 | tf_op jit(solution)/shard_map/ppermute | solution.py:952
  227.2 58.4 %collective-permute-start.10 = (bf16[1,3,2,384,256]{4,3,2,1,0:T(8,128)(2,1)}, bf16[1,3,2,384,256]{4,3,2,1,0:T(8,128)(2,1)}, u32[]{:S(2)}, u32[]{:S(2)}) collective-permute-start(bf16[1,3,2,384,256]{4,3,2,1,0:T(8,128)(2,1)} %get-tuple-element.170), channel_id=1, source_target_pairs={{0,8},{8,0},{16,24},{24,16},{1,9},{9,1},{17,25},{25,17},{2,10},{10... | collective-permute-start | bytes 3538952 | tf_op jit(solution)/shard_map/ppermute | solution.py:952
  228.7 57.0 %collective-permute-start.11 = (bf16[1,3,2,384,256]{4,3,2,1,0:T(8,128)(2,1)}, bf16[1,3,2,384,256]{4,3,2,1,0:T(8,128)(2,1)}, u32[]{:S(2)}, u32[]{:S(2)}) collective-permute-start(bf16[1,3,2,384,256]{4,3,2,1,0:T(8,128)(2,1)} %get-tuple-element.171), channel_id=1, source_target_pairs={{0,16},{8,24},{16,0},{24,8},{1,17},{9,25},{17,1},{25,9},{2,18},{10... | collective-permute-start | bytes 3538952 | tf_op jit(solution)/shard_map/ppermute | solution.py:952
  236.9 68.2 %all-to-all-start = ((bf16[4,192,1536]{2,1,0:T(8,128)(2,1)}), bf16[4,192,1536]{2,1,0:T(8,128)(2,1)S(1)}, u32[]{:S(2)}, u32[]{:S(2)}) async-start(bf16[4,192,1536]{2,1,0:T(8,128)(2,1)} %shard_map.245), calls=%async_computation | async-start | bytes 4718592 | tf_op jit(solution)/shard_map/all_to_all | solution.py:1102
  306.5 63.1 %all-to-all-start.1 = ((bf16[4,208,1536]{2,1,0:T(8,128)(2,1)}), bf16[4,208,1536]{2,1,0:T(8,128)(2,1)S(1)}, u32[]{:S(2)}, u32[]{:S(2)}) async-start(bf16[4,208,1536]{2,1,0:T(8,128)(2,1)} %shard_map.249), calls=%async_computation.1 | async-start | bytes 5111808 | tf_op jit(solution)/shard_map/all_to_all | solution.py:1111
  311.3 148.5 %all-gather.11.cloned.1.call-start = ((), (), s32[]{:S(2)}) async-start(), calls=%async_computation.7 | async-start | bytes 5750784 | tf_op jit(solution)/shard_map/all_gather | solution.py:936
  311.3 53.2 %collective-permute-start.15 = (bf16[2,3,2,384,256]{4,3,2,1,0:T(8,128)(2,1)}, bf16[2,3,2,384,256]{4,3,2,1,0:T(8,128)(2,1)S(1)}, u32[]{:S(2)}, u32[]{:S(2)}) collective-permute-start(bf16[2,3,2,384,256]{4,3,2,1,0:T(8,128)(2,1)} %get-tuple-element.183), channel_id=1, source_target_pairs={{0,8},{8,0},{16,24},{24,16},{1,9},{9,1},{17,25},{25,17},{2,10},{10... | collective-permute-start | bytes 7077896 | tf_op jit(solution)/shard_map/ppermute | solution.py:952
  311.7 53.3 %collective-permute-start.16 = (bf16[2,3,2,384,256]{4,3,2,1,0:T(8,128)(2,1)}, bf16[2,3,2,384,256]{4,3,2,1,0:T(8,128)(2,1)}, u32[]{:S(2)}, u32[]{:S(2)}) collective-permute-start(bf16[2,3,2,384,256]{4,3,2,1,0:T(8,128)(2,1)} %get-tuple-element.184), channel_id=1, source_target_pairs={{0,16},{8,24},{16,0},{24,8},{1,17},{9,25},{17,1},{25,9},{2,18},{10... | collective-permute-start | bytes 7077896 | tf_op jit(solution)/shard_map/ppermute | solution.py:952
  313.7 51.3 %collective-permute-start.14 = (bf16[2,4,80,1536]{3,2,1,0:T(8,128)(2,1)}, bf16[2,4,80,1536]{3,2,1,0:T(8,128)(2,1)}, u32[]{:S(2)}, u32[]{:S(2)}) collective-permute-start(bf16[2,4,80,1536]{3,2,1,0:T(8,128)(2,1)} %collective-permute-done.8.mine_b_ref), channel_id=1, source_target_pairs={{0,4},{4,0},{1,5},{5,1},{2,6},{6,2},{3,7},{7,3},{8,12},{12,8},{9,1... | collective-permute-start | bytes 5898248 | tf_op jit(solution)/shard_map/ppermute | solution.py:1131
  313.7 51.3 %collective-permute-start.13 = (bf16[2,4,80,1536]{3,2,1,0:T(8,128)(2,1)}, bf16[2,4,80,1536]{3,2,1,0:T(8,128)(2,1)}, u32[]{:S(2)}, u32[]{:S(2)}) collective-permute-start(bf16[2,4,80,1536]{3,2,1,0:T(8,128)(2,1)} %maximum_select_fusion.1.mine_a_ref), channel_id=1, source_target_pairs={{0,4},{4,0},{1,5},{5,1},{2,6},{6,2},{3,7},{7,3},{8,12},{12,8},{9,1... | collective-permute-start | bytes 5898248 | tf_op jit(solution)/shard_map/ppermute | solution.py:1131
  378.8 38.0 %all-to-all-start.2 = ((bf16[8,192,256]{2,1,0:T(8,128)(2,1)}), bf16[8,192,256]{2,1,0:T(8,128)(2,1)S(1)}, u32[]{:S(2)}, u32[]{:S(2)}) async-start(bf16[8,192,256]{2,1,0:T(8,128)(2,1)} %get-tuple-element.186), calls=%async_computation.2 | async-start | bytes 1572864 | tf_op jit(solution)/shard_map/all_to_all | solution.py:1142
  382.6 95.5 %collective-permute-start.21 = (bf16[2,3,2,384,256]{4,3,2,1,0:T(8,128)(2,1)}, bf16[2,3,2,384,256]{4,3,2,1,0:T(8,128)(2,1)}, u32[]{:S(2)}, u32[]{:S(2)}) collective-permute-start(bf16[2,3,2,384,256]{4,3,2,1,0:T(8,128)(2,1)} %get-tuple-element.218), channel_id=1, source_target_pairs={{0,8},{8,0},{16,24},{24,16},{1,9},{9,1},{17,25},{25,17},{2,10},{10... | collective-permute-start | bytes 7077896 | tf_op jit(solution)/shard_map/ppermute | solution.py:952
  383.0 95.1 %collective-permute-start.22 = (bf16[2,3,2,384,256]{4,3,2,1,0:T(8,128)(2,1)}, bf16[2,3,2,384,256]{4,3,2,1,0:T(8,128)(2,1)}, u32[]{:S(2)}, u32[]{:S(2)}) collective-permute-start(bf16[2,3,2,384,256]{4,3,2,1,0:T(8,128)(2,1)} %get-tuple-element.220), channel_id=1, source_target_pairs={{0,16},{8,24},{16,0},{24,8},{1,17},{9,25},{17,1},{25,9},{2,18},{10... | collective-permute-start | bytes 7077896 | tf_op jit(solution)/shard_map/ppermute | solution.py:952
  391.4 83.4 %collective-permute-start.19 = (bf16[3,3,384,256]{3,2,1,0:T(8,128)(2,1)}, bf16[3,3,384,256]{3,2,1,0:T(8,128)(2,1)}, u32[]{:S(2)}, u32[]{:S(2)}) collective-permute-start(bf16[3,3,384,256]{3,2,1,0:T(8,128)(2,1)} %get-tuple-element.215), channel_id=1, source_target_pairs={{0,16},{8,24},{16,0},{24,8},{1,17},{9,25},{17,1},{25,9},{2,18},{10... | collective-permute-start | bytes 5308424 | tf_op jit(solution)/shard_map/ppermute | solution.py:952
  392.5 82.4 %collective-permute-start.20 = (bf16[3,3,384,256]{3,2,1,0:T(8,128)(2,1)}, bf16[3,3,384,256]{3,2,1,0:T(8,128)(2,1)}, u32[]{:S(2)}, u32[]{:S(2)}) collective-permute-start(bf16[3,3,384,256]{3,2,1,0:T(8,128)(2,1)} %get-tuple-element.216), channel_id=1, source_target_pairs={{0,8},{8,0},{16,24},{24,16},{1,9},{9,1},{17,25},{25,17},{2,10},{10... | collective-permute-start | bytes 5308424 | tf_op jit(solution)/shard_map/ppermute | solution.py:952
  449.0 44.4 %all-to-all-start.3 = ((bf16[8,208,384]{2,1,0:T(8,128)(2,1)}), bf16[8,208,384]{2,1,0:T(8,128)(2,1)S(1)}, u32[]{:S(2)}, u32[]{:S(2)}) async-start(bf16[8,208,384]{2,1,0:T(8,128)(2,1)} %get-tuple-element.202), calls=%async_computation.3 | async-start | bytes 2555904 | tf_op jit(solution)/shard_map/all_to_all | solution.py:1151
  484.3 48.1 %collective-permute-start.29 = (bf16[2,3,384,256]{3,2,1,0:T(8,128)(2,1)}, bf16[2,3,384,256]{3,2,1,0:T(8,128)(2,1)S(1)}, u32[]{:S(2)}, u32[]{:S(2)}) collective-permute-start(bf16[2,3,384,256]{3,2,1,0:T(8,128)(2,1)} %get-tuple-element.234), channel_id=1, source_target_pairs={{0,16},{8,24},{16,0},{24,8},{1,17},{9,25},{17,1},{25,9},{2,18},{10... | collective-permute-start | bytes 3538952 | tf_op jit(solution)/shard_map/ppermute | solution.py:952
  484.6 47.9 %collective-permute-start.30 = (bf16[2,3,384,256]{3,2,1,0:T(8,128)(2,1)}, bf16[2,3,384,256]{3,2,1,0:T(8,128)(2,1)}, u32[]{:S(2)}, u32[]{:S(2)}) collective-permute-start(bf16[2,3,384,256]{3,2,1,0:T(8,128)(2,1)} %get-tuple-element.236), channel_id=1, source_target_pairs={{0,8},{8,0},{16,24},{24,16},{1,9},{9,1},{17,25},{25,17},{2,10},{10... | collective-permute-start | bytes 3538952 | tf_op jit(solution)/shard_map/ppermute | solution.py:952
  485.3 39.2 %collective-permute-start.28 = (f32[41,1536]{1,0:T(8,128)S(1)}, f32[41,1536]{1,0:T(8,128)S(1)}, u32[]{:S(2)}, u32[]{:S(2)}) collective-permute-start(f32[41,1536]{1,0:T(8,128)S(1)} %fusion.6), channel_id=1, source_target_pairs={{0,16},{8,24},{16,0},{24,8},{1,17},{9,25},{17,1},{25,9},{2,18},{10... | collective-permute-start | bytes 755720 | tf_op jit(solution)/shard_map/ppermute | solution.py:952
  (40 other events, 339.4 us)
Sparse Core Ops, SparseCore 0:
  9.7 54.3 all-gather.4
  98.5 53.2 all-gather.6
  153.4 52.7 all-gather.8
  378.9 67.2 all-gather.10
where the time goes:
time: 554 us; the launch traced here: 545 us
  Pallas kernels  241 us (44%)
  waiting for transfers between devices  179 us (32%)
  starting transfers between devices  63.1 us (11%)
  local copies, waits for them, and re-layouts  33.7 us (6%)
  between operations  14.7 us (3%)
  other arithmetic  13.7 us (2%)
    ppermute x23, waiting for transfers between devices, flip(): return lax.ppermute(value, axis, [(i, i ^ 1 << bit) for i in range(size)])  96.2 us
    pallas_call x3, Pallas kernels, run_experts_back(): call(lambda *refs: expert_back_kernel(*refs, fast=fast), (count,), 1, [ta...  45.9 us
    all_gather x4, waiting for transfers between devices, gather_group(): return lax.all_gather(block, ('row', 'col'), axis=0, tiled=True)  42.3 us
    pallas_call x1, Pallas kernels, attend_back(): call(attend_back_kernel, (total // QUERY_BLOCK,), 0, [whole(item.shape) f...  31.4 us
    ppermute x23, starting transfers between devices, flip(): return lax.ppermute(value, axis, [(i, i ^ 1 << bit) for i in range(size)])  25.5 us
    pallas_call x4, Pallas kernels, combine(): call(lambda *refs: combine_kernel(*refs, pieces=len(parts), with_dots=boo...  24.7 us
    pallas_call x1, Pallas kernels, run_experts(): call(expert_kernel, (count,), 0, [per_expert(slots, width), per_expert(sl...  23.5 us
    all_to_all x1, waiting for transfers between devices, local(): lax.all_to_all(attended_grad, ('row', 'col'), 0, 0, tiled=True)  21.8 us
  transfers between devices with their start and end apart: 39, of which 18 were waited for; matrix products, arithmetic and copies ran while one was open for 6% of the time, Pallas kernels for 42%

commit v1 on v0

--- a/solution.py
+++ b/solution.py
@@ -1130,10 +1130,8 @@
             gate_middle = ()
         w_in_parts += [lax.ppermute(after(part, back_mine), "row", SWAP) for part in w_in_parts]
 
-        mixed = (middle + jnp.sum(after(forth_sums, back_mine).astype(f32), axis=0)).astype(bf16)
-
         middle_grad, branch_grad, attended_grad = middle_back(
-            place, back_sums, gates, middle, cotangent, after(gain_two, mixed, *w_in_parts[2:], *gate_middle),
+            place, back_sums, gates, middle, cotangent, after(gain_two, *w_in_parts[2:], *gate_middle),
             w_router_rows, w_out_mine, w_out_other,
         )
         if fast:
@@ -1148,6 +1146,7 @@
         projected_grad, own_grads = attend_back(
             query, key, value, attended_grad, totals, start_row, cosine, sine, normed_one, w_natural, gain_column
         )
+        mixed = (middle + jnp.sum(after(forth_sums, own_grads).astype(f32), axis=0)).astype(bf16)
         projected_all = lax.all_to_all(projected_grad, ("row", "col"), 0, 0, tiled=True)
         *w_parts, small = out_weights(
             place, branch_all, attended, normed_two.reshape(group, width), own_grads,
@@ -1179,11 +1178,12 @@
             held_a, got_a, held_b, got_b = started[0]
             held_a, held_b = after((held_a, held_b), tokens_grad)
             expert_grads = last_sum(held_a, got_a, held_b, got_b, 0, local_experts, None)
-            share = share + flip(share, "dp", 0, n_dp)
+            share = share + after(flip(share, "dp", 0, n_dp), expert_grads[0])
             held_a, got_a, held_b, got_b = started[1]
-            held_a, held_b = after((held_a, held_b), share)
+            held_a, held_b = after((held_a, held_b), share, w_sums[1], w_sums[3])
             expert_grads = last_sum(held_a, got_a, held_b, got_b, cuts[2], local_experts, expert_grads)
-            gain_attn_grad = (share + flip(share, "dp", 1, n_dp)).reshape(width)
+            gain_attn_grad = share + after(flip(share, "dp", 1, n_dp), expert_grads[0])
+            gain_attn_grad = gain_attn_grad.reshape(width)
         else:
             gain_attn_grad = sum_dp(share, sizes).reshape(width)
 

time: 554 us -> 541 us (0.977)
  waiting for transfers between devices: 179 us -> 170 us
  starting transfers between devices: 63.1 us -> 54.4 us
    all_to_all x1, starting transfers between devices: 14.3 us -> 5.11 us  [local(): forth_sums = lax.all_to_all(forth_mine, 'col', 0, 0, tiled=True)]
    ppermute x23, waiting for transfers between devices: 96.2 us -> 89.1 us  [flip(): return lax.ppermute(value, axis, [(i, i ^ 1 << bit) for i in range(size)])]
    unnamed x61 -> x59, local copies, waits for them, and re-layouts: 16.8 us -> 16.9 us
  transfers between devices with their start and end apart: 39 -> 39, of which waited for: 18 -> 17; matrix products, arithmetic and copies ran while one was open for 6% -> 7% of each run, Pallas kernels for 42% -> 44%
where the time goes in v1:
time: 541 us; the launch traced here: 532 us
  Pallas kernels  241 us (45%)
  waiting for transfers between devices  170 us (31%)
  starting transfers between devices  54.4 us (10%)
  local copies, waits for them, and re-layouts  33.8 us (6%)
  other arithmetic  17.9 us (3%)
  between operations  14.7 us (3%)
    ppermute x23, waiting for transfers between devices, flip(): return lax.ppermute(value, axis, [(i, i ^ 1 << bit) for i in range(size)])  89.1 us
    pallas_call x3, Pallas kernels, run_experts_back(): call(lambda *refs: expert_back_kernel(*refs, fast=fast), (count,), 1, [ta...  45.9 us
    all_gather x4, waiting for transfers between devices, gather_group(): return lax.all_gather(block, ('row', 'col'), axis=0, tiled=True)  42.3 us
    pallas_call x1, Pallas kernels, attend_back(): call(attend_back_kernel, (total // QUERY_BLOCK,), 0, [whole(item.shape) f...  31.4 us
    ppermute x23, starting transfers between devices, flip(): return lax.ppermute(value, axis, [(i, i ^ 1 << bit) for i in range(size)])  25.7 us
    pallas_call x4, Pallas kernels, combine(): call(lambda *refs: combine_kernel(*refs, pieces=len(parts), with_dots=boo...  24.7 us
    pallas_call x1, Pallas kernels, run_experts(): call(expert_kernel, (count,), 0, [per_expert(slots, width), per_expert(sl...  23.5 us
    all_to_all x1, waiting for transfers between devices, local(): lax.all_to_all(attended_grad, ('row', 'col'), 0, 0, tiled=True)  21.7 us
  transfers between devices with their start and end apart: 39, of which 17 were waited for; matrix products, arithmetic and copies ran while one was open for 7% of the time, Pallas kernels for 44%

profile of v1, /device:TPU:0, one launch (start us, length us, event | category | flops | bytes accessed | tf_op | source)
XLA Modules:
  0.0 531.8 jit_solution(10416627627380435349)
XLA Ops:
  21.8 42.3 %all-gather.5.cloned.1.call-done.tok_ref.tok_a_ref.tok_b_ref = bf16[1536,1536]{1,0:T(8,128)(2,1)} async-done(((bf16[192,1536]{1,0:T(8,128)(2,1)}), bf16[1536,1536]{1,0:T(8,128)(2,1)}) %all-gather.5.cloned.1.call-update) | async-done | bytes 4718608 | tf_op jit(solution)/shard_map/all_gather | solution.py:936
  71.0 8.9 %shard_map.238 = (bf16[3,1536,128]{2,1,0:T(8,128)(2,1)}, bf16[1536,128]{1,0:T(8,128)(2,1)}, bf16[1536,128]{1,0:T(8,128)(2,1)}, bf16[1536,1536]{1,0:T(8,128)(2,1)}) custom-call(bf16[1536,1536]{1,0:T(8,128)(2,1)} %all-gather.5.cloned.1.call-done.tok_ref.tok_a_ref.tok_b_ref, f32[1,1536]{1,0:T(1,128)} %broadcast_in_dim.46.gain_ref, ...), custom_call_target="tpu_custom_call" | custom-call | flops 550000000 | bytes 1800000 | tf_op jit(solution)/shard_map/pallas_call | solution.py:115
  79.8 18.5 %shard_map.239 = (bf16[768,384]{1,0:T(8,128)(2,1)}, bf16[1536,256]{1,0:T(8,128)(2,1)}, f32[3,8,1536]{2,1,0:T(8,128)}) custom-call(bf16[3,1536,128]{2,1,0:T(8,128)(2,1)} %get-tuple-element.136.query_ref, bf16[1536,128]{1,0:T(8,128)(2,1)} %get-tuple-element.137.key_ref, bf16[1536,128]{1,0:T(8,128)(2,1)} %get-tuple-element.138.value_ref, s32[1536,1]{1,0:T(8,128)} %copy.55.start_ref), custom_call_target="tpu_custom_call" | custom-call | flops 550000000 | bytes 1800000 | tf_op jit(solution)/shard_map/pallas_call | solution.py:174
  107.8 12.8 %collective-permute-done.3 = bf16[1,4,48,1536]{3,2,1,0:T(8,128)(2,1)S(1)} collective-permute-done((bf16[1,4,48,1536]{3,2,1,0:T(8,128)(2,1)S(1)}, bf16[1,4,48,1536]{3,2,1,0:T(8,128)(2,1)S(1)}, u32[]{:S(2)}, u32[]{:S(2)}) %collective-permute-start.3) | collective-permute-done | bytes 589856 | tf_op jit(solution)/shard_map/ppermute | solution.py:952
  122.4 17.9 %collective-permute-done.5 = bf16[1,4,80,1536]{3,2,1,0:T(8,128)(2,1)} collective-permute-done((bf16[1,4,80,1536]{3,2,1,0:T(8,128)(2,1)S(1)}, bf16[1,4,80,1536]{3,2,1,0:T(8,128)(2,1)}, u32[]{:S(2)}, u32[]{:S(2)}) %collective-permute-start.5) | collective-permute-done | bytes 983072 | tf_op jit(solution)/shard_map/ppermute | solution.py:952
  157.8 21.6 %shard_map.240 = (bf16[5,2,4,64,1536]{4,3,2,1,0:T(8,128)(2,1)}, f32[5,2,4,64,128]{4,3,2,1,0:T(8,128)}, f32[2,4,8,192]{3,2,1,0:T(8,128)}, f32[2,4,8,192]{3,2,1,0:...) custom-call(s32[5]{0:T(128)} %stack.42.place_ref.refs_0_, ...), custom_call_target="tpu_custom_call" | custom-call | flops 550000000 | bytes 1800000 | tf_op jit(solution)/shard_map/pallas_call | solution.py:402
  179.3 23.5 %shard_map.241 = (bf16[5,512,1536]{2,1,0:T(8,128)(2,1)}, bf16[5,512,512]{2,1,0:T(8,128)(2,1)}, f32[5,512,512]{2,1,0:T(8,128)}, f32[5,512,512]{2,1,0:T(8,128)}) custom-call(bf16[5,512,1536]{2,1,0:T(8,128)(2,1)} %bitcast.73, f32[5,512,128]{2,1,0:T(8,128)} %bitcast.109, bf16[5,1536,512]{2,1,0:T(8,128)(2,1)} %refs_6_.5, bf16[5,1536,512]{2,1,0:T(8,128)(2,1)} %refs_7_.5, ...), custom_call_target="tpu_custom_call" | custom-call | flops 550000000 | bytes 1800000 | tf_op jit(solution)/shard_map/pallas_call | solution.py:493
  208.7 7.2 %shard_map.243 = bf16[5,8,64,1536]{3,2,1,0:T(8,128)(2,1)} custom-call(f32[8,8,192]{2,1,0:T(8,128)} %bitcast.105, f32[8,8,192]{2,1,0:T(8,128)} %bitcast.114, bf16[1536,1536]{1,0:T(8,128)(2,1)} %all-gather.9.cloned.1.call-done.cot_ref), custom_call_target="tpu_custom_call" | custom-call | flops 550000000 | bytes 1800000 | tf_op jit(solution)/shard_map/pallas_call | solution.py:461
  216.0 11.4 %shard_map.244 = (bf16[1,512,1536]{2,1,0:T(8,128)(2,1)}, f32[1,512,128]{2,1,0:T(8,128)}, bf16[1,3,2,384,256]{4,3,2,1,0:T(8,128)(2,1)}, bf16[1,3,2,384,256]{4,3,2...) custom-call(s32[5]{0:T(128)} %stack.42.place_ref.refs_0_, ...), custom_call_target="tpu_custom_call" | custom-call | flops 550000000 | bytes 1800000 | tf_op jit(solution)/shard_map/pallas_call | solution.py:570
  230.8 6.3 %shard_map.245 = bf16[4,192,1536]{2,1,0:T(8,128)(2,1)} custom-call(s32[5]{0:T(128)} %stack.42.place_ref.refs_0_, f32[8,8,192]{2,1,0:T(8,128)} %bitcast.106, bf16[5,8,64,1536]{3,2,1,0:T(8,128)(2,1)} %bitcast.78, bf16[4,192,1536]{2,1,0:T(8,128)(2,1)} %copy-done.12), custom_call_target="tpu_custom_call" | custom-call | flops 550000000 | bytes 1800000 | tf_op jit(solution)/shard_map/pallas_call | solution.py:632
  242.2 17.2 %shard_map.246 = (bf16[2,512,1536]{2,1,0:T(8,128)(2,1)}, f32[2,512,128]{2,1,0:T(8,128)}, bf16[2,3,2,384,256]{4,3,2,1,0:T(8,128)(2,1)}, bf16[2,3,2,384,256]{4,3,2...) custom-call(s32[5]{0:T(128)} %stack.42.place_ref.refs_0_, ...), custom_call_target="tpu_custom_call" | custom-call | flops 550000000 | bytes 1800000 | tf_op jit(solution)/shard_map/pallas_call | solution.py:570
  259.4 17.2 %shard_map.247 = (bf16[2,512,1536]{2,1,0:T(8,128)(2,1)}, f32[2,512,128]{2,1,0:T(8,128)}, bf16[2,3,2,384,256]{4,3,2,1,0:T(8,128)(2,1)}, bf16[2,3,2,384,256]{4,3,2...) custom-call(s32[5]{0:T(128)} %stack.42.place_ref.refs_0_, ...), custom_call_target="tpu_custom_call" | custom-call | flops 550000000 | bytes 1800000 | tf_op jit(solution)/shard_map/pallas_call | solution.py:570
  276.7 6.0 %shard_map.248 = bf16[4,208,1536]{2,1,0:T(8,128)(2,1)} custom-call(s32[5]{0:T(128)} %stack.42.place_ref.refs_0_, f32[8,8,192]{2,1,0:T(8,128)} %bitcast.107, bf16[1,8,64,1536]{3,2,1,0:T(8,128)(2,1)} %bitcast.88, bf16[2,8,64,1536]{3,2,1,0:T(8,128)(2,1)} %bitcast.84, bf16[2,8,64,1536]{3,2,1,0:T(8,128)(2,1)} %bitcast.86, f32[1,8,64,128]{3,2,1,0:T(8,128)} %bitcast.110, ...), custom_call_target="tpu_custom_call" | custom-call | flops 550000000 | bytes 1800000 | tf_op jit(solution)/shard_map/pallas_call | solution.py:632
  289.1 6.7 %shard_map.249 = bf16[4,208,1536]{2,1,0:T(8,128)(2,1)} custom-call(s32[5]{0:T(128)} %stack.42.place_ref.refs_0_, f32[8,8,192]{2,1,0:T(8,128)} %bitcast.108, bf16[1,8,64,1536]{3,2,1,0:T(8,128)(2,1)} %bitcast.89, bf16[2,8,64,1536]{3,2,1,0:T(8,128)(2,1)} %bitcast.85, bf16[2,8,64,1536]{3,2,1,0:T(8,128)(2,1)} %bitcast.87, f32[1,8,64,128]{3,2,1,0:T(8,128)} %bitcast.111, ...), custom_call_target="tpu_custom_call" | custom-call | flops 550000000 | bytes 1800000 | tf_op jit(solution)/shard_map/pallas_call | solution.py:632
  310.1 45.4 %collective-permute-done.15.got_a_ref = bf16[2,3,2,384,256]{4,3,2,1,0:T(8,128)(2,1)S(1)} collective-permute-done((bf16[2,3,2,384,256]{4,3,2,1,0:T(8,128)(2,1)}, bf16[2,3,2,384,256]{4,3,2,1,0:T(8,128)(2,1)S(1)}, u32[]{:S(2)}, u32[]{:S(2)}) %collective-permute-start.15) | collective-permute-done | bytes 2359328 | tf_op jit(solution)/shard_map/ppermute | solution.py:952
  362.1 7.7 %shard_map.251 = (f32[192,1536]{1,0:T(8,128)}, bf16[208,1536]{1,0:T(8,128)(2,1)}, bf16[8,192,256]{2,1,0:T(8,128)(2,1)}) custom-call(s32[5]{0:T(128)} %stack.42.place_ref.refs_0_, bf16[4,208,1536]{2,1,0:T(8,128)(2,1)} %copy-done.4, f32[64,192]{1,0:T(8,128)} %get-tuple-element.176.gates_ref, f32[192,1536]{1,0:T(8,128)} %get-tuple-element.150.middle_ref, ...), custom_call_target="tpu_custom_call" | custom-call | flops 550000000 | bytes 1800000 | tf_op jit(solution)/shard_map/pallas_call | solution.py:705
  376.0 6.4 %shard_map.252 = (bf16[3,3,384,256]{3,2,1,0:T(8,128)(2,1)}, bf16[3,3,384,256]{3,2,1,0:T(8,128)(2,1)}, bf16[3,3,384,256]{3,2,1,0:T(8,128)(2,1)}, bf16[3,3,384,256]{3,2,1,0:T(8,128)(2,1)}) custom-call(s32[5]{0:T(128)} %stack.42.place_ref.refs_0_, ...), custom_call_target="tpu_custom_call", output_to_operand_aliasing={{0}: (5, {}), {1}: (6, {}), {2}: (7, {}), {3}: (8, {})} | custom-call | flops 550000000 | bytes 1800000 | tf_op jit(solution)/shard_map/pallas_call | solution.py:867
  386.0 21.7 %all-to-all-done.2 = bf16[8,192,256]{2,1,0:T(8,128)(2,1)S(1)} async-done(((bf16[8,192,256]{2,1,0:T(8,128)(2,1)}), bf16[8,192,256]{2,1,0:T(8,128)(2,1)S(1)}, u32[]{:S(2)}, u32[]{:S(2)}) %all-to-all-start.2) | async-done | bytes 786464 | tf_op jit(solution)/shard_map/all_to_all | solution.py:1140
  408.6 31.4 %shard_map.253 = (bf16[8,208,384]{2,1,0:T(8,128)(2,1)}, bf16[1536,384]{1,0:T(8,128)(2,1)}) custom-call(bf16[3,1536,128]{2,1,0:T(8,128)(2,1)} %get-tuple-element.136.query_ref, bf16[1536,128]{1,0:T(8,128)(2,1)} %get-tuple-element.137.key_ref, bf16[1536,128]{1,0:T(8,128)(2,1)} %get-tuple-element.138.value_ref, bf16[1536,256]{1,0:T(8,128)(2,1)} %bitcast.95, ...), custom_call_target="tpu_custom_call" | custom-call | flops 550000000 | bytes 1800000 | tf_op jit(solution)/shard_map/pallas_call | solution.py:283
  440.1 10.8 %all-to-all-start.3 = ((bf16[8,208,384]{2,1,0:T(8,128)(2,1)}), bf16[8,208,384]{2,1,0:T(8,128)(2,1)S(1)}, u32[]{:S(2)}, u32[]{:S(2)}) async-start(bf16[8,208,384]{2,1,0:T(8,128)(2,1)} %get-tuple-element.205), calls=%async_computation.3 | async-start | bytes 2555904 | tf_op jit(solution)/shard_map/all_to_all | solution.py:1150
  454.0 8.8 %shard_map.254 = (bf16[1,1,2,384,256]{4,3,2,1,0:T(8,128)(2,1)}, bf16[1,1,2,384,256]{4,3,2,1,0:T(8,128)(2,1)}, bf16[1,1,2,384,256]{4,3,2,1,0:T(8,128)(2,1)}, bf16...) custom-call(s32[5]{0:T(128)} %stack.42.place_ref.refs_0_, bf16[1664,1536]{1,0:T(8,128)(2,1)} %all-gather.11.cloned.1.call-done.refs_1_, ...), custom_call_target="tpu_custom_call" | custom-call | flops 550000000 | bytes 1800000 | tf_op jit(solution)/shard_map/pallas_call | solution.py:833
  470.8 6.4 %shard_map.256 = (bf16[2,3,384,256]{3,2,1,0:T(8,128)(2,1)}, bf16[2,3,384,256]{3,2,1,0:T(8,128)(2,1)}, bf16[2,3,384,256]{3,2,1,0:T(8,128)(2,1)}, bf16[2,3,384,256]{3,2,1,0:T(8,128)(2,1)}) custom-call(s32[5]{0:T(128)} %stack.42.place_ref.refs_0_, bf16[2,3,2,384,256]{4,3,2,1,0:T(8,128)(2,1)} %get-tuple-element.219.keep_a_ref, ...), custom_call_target="tpu_custom_call" | custom-call | flops 550000000 | bytes 1800000 | tf_op jit(solution)/shard_map/pallas_call | solution.py:867
  489.7 8.9 %shard_map.257 = (f32[192,1536]{1,0:T(8,128)}, f32[8,384]{1,0:T(8,128)}) custom-call(s32[5]{0:T(128)} %stack.42.place_ref.refs_0_, bf16[8,208,384]{2,1,0:T(8,128)(2,1)} %copy-done.3, bf16[8,208,384]{2,1,0:T(8,128)(2,1)} %copy-done.3, bf16[2,4,80,1536]{3,2,1,0:T(8,128)(2,1)} %maximum_select_fusion.1.mine_a_ref, ...), custom_call_target="tpu_custom_call" | custom-call | flops 550000000 | bytes 1800000 | tf_op jit(solution)/shard_map/pallas_call | solution.py:764
  500.0 6.8 %shard_map.258 = (f32[5,384,512]{2,1,0:T(8,128)}, f32[5,384,512]{2,1,0:T(8,128)}, f32[5,384,512]{2,1,0:T(8,128)}) custom-call(bf16[3,3,384,256]{3,2,1,0:T(8,128)(2,1)} %get-tuple-element.228.held_a_ref, bf16[3,3,384,256]{3,2,1,0:T(8,128)(2,1)} %collective-permute-done.19.got_a_ref, bf16[3,3,384,256]{3,2,1,0:T(8,128)(2,1)} %get-tuple-element.229.held_b_ref, ...), custom_call_target="tpu_custom_call" | custom-call | flops 550000000 | bytes 1800000 | tf_op jit(solution)/shard_map/pallas_call | solution.py:892
  (192 shorter events, 145.4 us)
Async XLA Ops:
  7.2 56.9 %all-gather.5.cloned.1.call-start = ((), (), s32[]{:S(2)}) async-start(), calls=%async_computation.4 | async-start | bytes 5308416 | tf_op jit(solution)/shard_map/all_gather | solution.py:936
  8.0 149.8 %all-gather.7.cloned.1.call-start = ((), (), s32[]{:S(2)}) async-start(), calls=%async_computation.5 | async-start | bytes 5308416 | tf_op jit(solution)/shard_map/all_gather | solution.py:936
  65.0 37.3 %collective-permute-start.1 = (bf16[136,1536]{1,0:T(8,128)(2,1)S(1)}, bf16[136,1536]{1,0:T(8,128)(2,1)S(1)}, u32[]{:S(2)}, u32[]{:S(2)}) collective-permute-start(bf16[136,1536]{1,0:T(8,128)(2,1)S(1)} %fusion.2), channel_id=1, source_target_pairs={{0,2},{1,3},{2,0},{3,1},{4,6},{5,7},{6,4},{7,5},{8,10},{9,11},{10,... | collective-permute-start | bytes 1253384 | tf_op jit(solution)/shard_map/ppermute | solution.py:942
  65.5 36.7 %collective-permute-start.2 = (bf16[136,1536]{1,0:T(8,128)(2,1)S(1)}, bf16[136,1536]{1,0:T(8,128)(2,1)S(1)}, u32[]{:S(2)}, u32[]{:S(2)}) collective-permute-start(bf16[136,1536]{1,0:T(8,128)(2,1)S(1)} %fusion.2), channel_id=1, source_target_pairs={{0,1},{1,2},{2,3},{3,0},{4,5},{5,6},{6,7},{7,4},{8,9},{9,10},{10,1... | collective-permute-start | bytes 1253384 | tf_op jit(solution)/shard_map/ppermute | solution.py:942
  98.4 110.3 %all-gather.9.cloned.1.call-start = ((), (), s32[]{:S(2)}) async-start(), calls=%async_computation.6 | async-start | bytes 5308416 | tf_op jit(solution)/shard_map/all_gather | solution.py:936
  153.3 49.5 %collective-permute-start.8 = (bf16[2,4,80,1536]{3,2,1,0:T(8,128)(2,1)}, bf16[2,4,80,1536]{3,2,1,0:T(8,128)(2,1)}, u32[]{:S(2)}, u32[]{:S(2)}) collective-permute-start(bf16[2,4,80,1536]{3,2,1,0:T(8,128)(2,1)} %maximum_select_fusion.1.mine_a_ref), channel_id=1, source_target_pairs={{0,16},{8,24},{16,0},{24,8},{1,17},{9,25},{17,1},{25,9},{2,18},{10... | collective-permute-start | bytes 5898248 | tf_op jit(solution)/shard_map/ppermute | solution.py:952
  227.4 49.3 %collective-permute-start.10 = (bf16[1,3,2,384,256]{4,3,2,1,0:T(8,128)(2,1)}, bf16[1,3,2,384,256]{4,3,2,1,0:T(8,128)(2,1)}, u32[]{:S(2)}, u32[]{:S(2)}) collective-permute-start(bf16[1,3,2,384,256]{4,3,2,1,0:T(8,128)(2,1)} %get-tuple-element.172), channel_id=1, source_target_pairs={{0,8},{8,0},{16,24},{24,16},{1,9},{9,1},{17,25},{25,17},{2,10},{10... | collective-permute-start | bytes 3538952 | tf_op jit(solution)/shard_map/ppermute | solution.py:952
  228.8 47.8 %collective-permute-start.11 = (bf16[1,3,2,384,256]{4,3,2,1,0:T(8,128)(2,1)}, bf16[1,3,2,384,256]{4,3,2,1,0:T(8,128)(2,1)}, u32[]{:S(2)}, u32[]{:S(2)}) collective-permute-start(bf16[1,3,2,384,256]{4,3,2,1,0:T(8,128)(2,1)} %get-tuple-element.173), channel_id=1, source_target_pairs={{0,16},{8,24},{16,0},{24,8},{1,17},{9,25},{17,1},{25,9},{2,18},{10... | collective-permute-start | bytes 3538952 | tf_op jit(solution)/shard_map/ppermute | solution.py:952
  237.1 58.9 %all-to-all-start = ((bf16[4,192,1536]{2,1,0:T(8,128)(2,1)}), bf16[4,192,1536]{2,1,0:T(8,128)(2,1)S(1)}, u32[]{:S(2)}, u32[]{:S(2)}) async-start(bf16[4,192,1536]{2,1,0:T(8,128)(2,1)} %shard_map.245), calls=%async_computation | async-start | bytes 4718592 | tf_op jit(solution)/shard_map/all_to_all | solution.py:1102
  297.3 63.3 %all-to-all-start.1 = ((bf16[4,208,1536]{2,1,0:T(8,128)(2,1)}), bf16[4,208,1536]{2,1,0:T(8,128)(2,1)S(1)}, u32[]{:S(2)}, u32[]{:S(2)}) async-start(bf16[4,208,1536]{2,1,0:T(8,128)(2,1)} %shard_map.249), calls=%async_computation.1 | async-start | bytes 5111808 | tf_op jit(solution)/shard_map/all_to_all | solution.py:1111
  302.3 151.7 %all-gather.11.cloned.1.call-start = ((), (), s32[]{:S(2)}) async-start(), calls=%async_computation.7 | async-start | bytes 5750784 | tf_op jit(solution)/shard_map/all_gather | solution.py:936
  302.3 53.2 %collective-permute-start.15 = (bf16[2,3,2,384,256]{4,3,2,1,0:T(8,128)(2,1)}, bf16[2,3,2,384,256]{4,3,2,1,0:T(8,128)(2,1)S(1)}, u32[]{:S(2)}, u32[]{:S(2)}) collective-permute-start(bf16[2,3,2,384,256]{4,3,2,1,0:T(8,128)(2,1)} %get-tuple-element.184), channel_id=1, source_target_pairs={{0,8},{8,0},{16,24},{24,16},{1,9},{9,1},{17,25},{25,17},{2,10},{10... | collective-permute-start | bytes 7077896 | tf_op jit(solution)/shard_map/ppermute | solution.py:952
  302.7 53.2 %collective-permute-start.16 = (bf16[2,3,2,384,256]{4,3,2,1,0:T(8,128)(2,1)}, bf16[2,3,2,384,256]{4,3,2,1,0:T(8,128)(2,1)S(1)}, u32[]{:S(2)}, u32[]{:S(2)}) collective-permute-start(bf16[2,3,2,384,256]{4,3,2,1,0:T(8,128)(2,1)} %get-tuple-element.185), channel_id=1, source_target_pairs={{0,16},{8,24},{16,0},{24,8},{1,17},{9,25},{17,1},{25,9},{2,18},{10... | collective-permute-start | bytes 7077896 | tf_op jit(solution)/shard_map/ppermute | solution.py:952
  304.7 51.2 %collective-permute-start.14 = (bf16[2,4,80,1536]{3,2,1,0:T(8,128)(2,1)}, bf16[2,4,80,1536]{3,2,1,0:T(8,128)(2,1)}, u32[]{:S(2)}, u32[]{:S(2)}) collective-permute-start(bf16[2,4,80,1536]{3,2,1,0:T(8,128)(2,1)} %collective-permute-done.8.mine_b_ref), channel_id=1, source_target_pairs={{0,4},{4,0},{1,5},{5,1},{2,6},{6,2},{3,7},{7,3},{8,12},{12,8},{9,1... | collective-permute-start | bytes 5898248 | tf_op jit(solution)/shard_map/ppermute | solution.py:1131
  304.7 51.2 %collective-permute-start.13 = (bf16[2,4,80,1536]{3,2,1,0:T(8,128)(2,1)}, bf16[2,4,80,1536]{3,2,1,0:T(8,128)(2,1)}, u32[]{:S(2)}, u32[]{:S(2)}) collective-permute-start(bf16[2,4,80,1536]{3,2,1,0:T(8,128)(2,1)} %maximum_select_fusion.1.mine_a_ref), channel_id=1, source_target_pairs={{0,4},{4,0},{1,5},{5,1},{2,6},{6,2},{3,7},{7,3},{8,12},{12,8},{9,1... | collective-permute-start | bytes 5898248 | tf_op jit(solution)/shard_map/ppermute | solution.py:1131
  369.8 38.0 %all-to-all-start.2 = ((bf16[8,192,256]{2,1,0:T(8,128)(2,1)}), bf16[8,192,256]{2,1,0:T(8,128)(2,1)S(1)}, u32[]{:S(2)}, u32[]{:S(2)}) async-start(bf16[8,192,256]{2,1,0:T(8,128)(2,1)} %get-tuple-element.187), calls=%async_computation.2 | async-start | bytes 1572864 | tf_op jit(solution)/shard_map/all_to_all | solution.py:1140
  373.6 97.2 %collective-permute-start.21 = (bf16[2,3,2,384,256]{4,3,2,1,0:T(8,128)(2,1)}, bf16[2,3,2,384,256]{4,3,2,1,0:T(8,128)(2,1)}, u32[]{:S(2)}, u32[]{:S(2)}) collective-permute-start(bf16[2,3,2,384,256]{4,3,2,1,0:T(8,128)(2,1)} %get-tuple-element.220), channel_id=1, source_target_pairs={{0,8},{8,0},{16,24},{24,16},{1,9},{9,1},{17,25},{25,17},{2,10},{10... | collective-permute-start | bytes 7077896 | tf_op jit(solution)/shard_map/ppermute | solution.py:952
  374.0 96.8 %collective-permute-start.22 = (bf16[2,3,2,384,256]{4,3,2,1,0:T(8,128)(2,1)}, bf16[2,3,2,384,256]{4,3,2,1,0:T(8,128)(2,1)}, u32[]{:S(2)}, u32[]{:S(2)}) collective-permute-start(bf16[2,3,2,384,256]{4,3,2,1,0:T(8,128)(2,1)} %get-tuple-element.222), channel_id=1, source_target_pairs={{0,16},{8,24},{16,0},{24,8},{1,17},{9,25},{17,1},{25,9},{2,18},{10... | collective-permute-start | bytes 7077896 | tf_op jit(solution)/shard_map/ppermute | solution.py:952
  382.5 84.8 %collective-permute-start.19 = (bf16[3,3,384,256]{3,2,1,0:T(8,128)(2,1)}, bf16[3,3,384,256]{3,2,1,0:T(8,128)(2,1)}, u32[]{:S(2)}, u32[]{:S(2)}) collective-permute-start(bf16[3,3,384,256]{3,2,1,0:T(8,128)(2,1)} %get-tuple-element.217), channel_id=1, source_target_pairs={{0,16},{8,24},{16,0},{24,8},{1,17},{9,25},{17,1},{25,9},{2,18},{10... | collective-permute-start | bytes 5308424 | tf_op jit(solution)/shard_map/ppermute | solution.py:952
  383.6 85.4 %collective-permute-start.20 = (bf16[3,3,384,256]{3,2,1,0:T(8,128)(2,1)}, bf16[3,3,384,256]{3,2,1,0:T(8,128)(2,1)}, u32[]{:S(2)}, u32[]{:S(2)}) collective-permute-start(bf16[3,3,384,256]{3,2,1,0:T(8,128)(2,1)} %get-tuple-element.218), channel_id=1, source_target_pairs={{0,8},{8,0},{16,24},{24,16},{1,9},{9,1},{17,25},{25,17},{2,10},{10... | collective-permute-start | bytes 5308424 | tf_op jit(solution)/shard_map/ppermute | solution.py:952
  440.1 48.6 %all-to-all-start.3 = ((bf16[8,208,384]{2,1,0:T(8,128)(2,1)}), bf16[8,208,384]{2,1,0:T(8,128)(2,1)S(1)}, u32[]{:S(2)}, u32[]{:S(2)}) async-start(bf16[8,208,384]{2,1,0:T(8,128)(2,1)} %get-tuple-element.205), calls=%async_computation.3 | async-start | bytes 2555904 | tf_op jit(solution)/shard_map/all_to_all | solution.py:1150
  477.2 42.0 %collective-permute-start.27 = (bf16[2,3,384,256]{3,2,1,0:T(8,128)(2,1)}, bf16[2,3,384,256]{3,2,1,0:T(8,128)(2,1)S(1)}, u32[]{:S(2)}, u32[]{:S(2)}) collective-permute-start(bf16[2,3,384,256]{3,2,1,0:T(8,128)(2,1)} %get-tuple-element.236), channel_id=1, source_target_pairs={{0,16},{8,24},{16,0},{24,8},{1,17},{9,25},{17,1},{25,9},{2,18},{10... | collective-permute-start | bytes 3538952 | tf_op jit(solution)/shard_map/ppermute | solution.py:952
  477.4 41.8 %collective-permute-start.28 = (bf16[2,3,384,256]{3,2,1,0:T(8,128)(2,1)}, bf16[2,3,384,256]{3,2,1,0:T(8,128)(2,1)}, u32[]{:S(2)}, u32[]{:S(2)}) collective-permute-start(bf16[2,3,384,256]{3,2,1,0:T(8,128)(2,1)} %get-tuple-element.238), channel_id=1, source_target_pairs={{0,8},{8,0},{16,24},{24,16},{1,9},{9,1},{17,25},{25,17},{2,10},{10... | collective-permute-start | bytes 3538952 | tf_op jit(solution)/shard_map/ppermute | solution.py:952
  477.9 34.7 %collective-permute-start.30 = (f32[41,1536]{1,0:T(8,128)S(1)}, f32[41,1536]{1,0:T(8,128)S(1)}, u32[]{:S(2)}, u32[]{:S(2)}) collective-permute-start(f32[41,1536]{1,0:T(8,128)S(1)} %fusion.6), channel_id=1, source_target_pairs={{0,16},{8,24},{16,0},{24,8},{1,17},{9,25},{17,1},{25,9},{2,18},{10... | collective-permute-start | bytes 755720 | tf_op jit(solution)/shard_map/ppermute | solution.py:952
  (39 other events, 345.0 us)
Sparse Core Ops, SparseCore 0:
  9.7 54.3 all-gather.4
  98.5 51.8 all-gather.6
  153.4 52.9 all-gather.8
  369.9 67.2 all-gather.10

commit v2 on v1

--- a/solution.py
+++ b/solution.py
@@ -153,7 +153,8 @@
                 total_ref[number, :, rows] = jnp.transpose(total)[0:8, :]
                 return carry
 
-            lax.fori_loop(0, 3, head, 0)
+            for number in range(3):
+                head(number, 0)
             low = lane_of((QUERY_BLOCK, LANES)) < HEAD_DIM
             one, two, three = out_ref[0], out_ref[1], out_ref[2]
             pair = jnp.where(low, one, two).astype(bf16)
@@ -216,8 +217,8 @@
 
             def head(number, carry):
                 query = query_ref[number, rows, :]
-                tile = pl.multiple_of((number // 2) * LANES, LANES)
-                upstream = grad_ref[rows, pl.ds(tile, LANES)].astype(f32)
+                tile = number // 2 * LANES
+                upstream = grad_ref[rows, tile : tile + LANES].astype(f32)
                 keep = low == (number != 1)
                 upstream = jnp.where(keep, upstream, 0.0).astype(bf16)
                 scores = dot_nt(key_ref[0:span, :], query)
@@ -231,7 +232,8 @@
                 query_grad_ref[number] = dot_tn(score_grad, key_ref[0:span, :]) * scale
                 return carry
 
-            lax.fori_loop(0, 3, head, 0)
+            for number in range(3):
+                head(number, 0)
             cosine, sine = cos_ref[rows, :], sin_ref[rows, :]
             pair = jnp.where(low, query_grad_ref[0], query_grad_ref[1])
             out_ref[rows, 0:LANES] = back(pair, cosine, sine).astype(bf16)
@@ -1146,7 +1148,6 @@
         projected_grad, own_grads = attend_back(
             query, key, value, attended_grad, totals, start_row, cosine, sine, normed_one, w_natural, gain_column
         )
-        mixed = (middle + jnp.sum(after(forth_sums, own_grads).astype(f32), axis=0)).astype(bf16)
         projected_all = lax.all_to_all(projected_grad, ("row", "col"), 0, 0, tiled=True)
         *w_parts, small = out_weights(
             place, branch_all, attended, normed_two.reshape(group, width), own_grads,
@@ -1165,6 +1166,7 @@
             w_sum = reduce_over_dp(cut, n_dp)[0]
 
 
+        mixed = (middle + jnp.sum(after(forth_sums, small).astype(f32), axis=0)).astype(bf16)
         used = small.reshape(members, 8, width)[:, :local_experts].reshape(members * local_experts, width)
         both = sum_dp(jnp.concatenate([used, small[7:8]], axis=0), sizes)
         w_router_grad = both[: members * local_experts].T

time: 541 us -> 530 us (0.980)
  waiting for transfers between devices: 170 us -> 183 us
  starting transfers between devices: 54.4 us -> 47.3 us
  Pallas kernels: 241 us -> 234 us
    all_to_all x1, waiting for transfers between devices: 21.7 us -> 29.6 us  [local(): lax.all_to_all(attended_grad, ('row', 'col'), 0, 0, tiled=True)]
    all_to_all x1, starting transfers between devices: 10.8 us -> 4.39 us  [local(): lax.all_to_all(projected_grad, ('row', 'col'), 0, 0, tiled=True)]
    unnamed x59 -> x57, local copies, waits for them, and re-layouts: 16.9 us -> 16 us
  transfers between devices with their start and end apart: 39 -> 39, of which waited for: 17 -> 18; matrix products, arithmetic and copies ran while one was open for 7% -> 6% of each run, Pallas kernels for 44% -> 43%
where the time goes in v2:
time: 530 us; the launch traced here: 525 us
  Pallas kernels  234 us (44%)
  waiting for transfers between devices  183 us (35%)
  starting transfers between devices  47.3 us (9%)
  local copies, waits for them, and re-layouts  32.6 us (6%)
  between operations  14.5 us (3%)
  other arithmetic  13.9 us (3%)
    ppermute x23, waiting for transfers between devices, flip(): return lax.ppermute(value, axis, [(i, i ^ 1 << bit) for i in range(size)])  90.3 us
    pallas_call x3, Pallas kernels, run_experts_back(): call(lambda *refs: expert_back_kernel(*refs, fast=fast), (count,), 1, [ta...  46 us
    all_gather x4, waiting for transfers between devices, gather_group(): return lax.all_gather(block, ('row', 'col'), axis=0, tiled=True)  42.3 us
    all_to_all x1, waiting for transfers between devices, local(): lax.all_to_all(attended_grad, ('row', 'col'), 0, 0, tiled=True)  29.6 us
    pallas_call x1, Pallas kernels, attend_back(): call(attend_back_kernel, (total // QUERY_BLOCK,), 0, [whole(item.shape) f...  27.6 us
    ppermute x23, starting transfers between devices, flip(): return lax.ppermute(value, axis, [(i, i ^ 1 << bit) for i in range(size)])  25.3 us
    pallas_call x4, Pallas kernels, combine(): call(lambda *refs: combine_kernel(*refs, pieces=len(parts), with_dots=boo...  24.7 us
    pallas_call x1, Pallas kernels, run_experts(): call(expert_kernel, (count,), 0, [per_expert(slots, width), per_expert(sl...  23.6 us
  transfers between devices with their start and end apart: 39, of which 18 were waited for; matrix products, arithmetic and copies ran while one was open for 6% of the time, Pallas kernels for 43%

profile of v2, /device:TPU:0, one launch (start us, length us, event | category | flops | bytes accessed | tf_op | source)
XLA Modules:
  0.0 525.1 jit_solution(14889218647622297232)
XLA Ops:
  21.9 42.3 %all-gather.5.cloned.1.call-done.tok_ref.tok_a_ref.tok_b_ref = bf16[1536,1536]{1,0:T(8,128)(2,1)} async-done(((bf16[192,1536]{1,0:T(8,128)(2,1)}), bf16[1536,1536]{1,0:T(8,128)(2,1)}) %all-gather.5.cloned.1.call-update) | async-done | bytes 4718608 | tf_op jit(solution)/shard_map/all_gather | solution.py:938
  70.9 9.2 %shard_map.238 = (bf16[3,1536,128]{2,1,0:T(8,128)(2,1)}, bf16[1536,128]{1,0:T(8,128)(2,1)}, bf16[1536,128]{1,0:T(8,128)(2,1)}, bf16[1536,1536]{1,0:T(8,128)(2,1)}) custom-call(bf16[1536,1536]{1,0:T(8,128)(2,1)} %all-gather.5.cloned.1.call-done.tok_ref.tok_a_ref.tok_b_ref, f32[1,1536]{1,0:T(1,128)} %broadcast_in_dim.46.gain_ref, ...), custom_call_target="tpu_custom_call" | custom-call | flops 550000000 | bytes 1800000 | tf_op jit(solution)/shard_map/pallas_call | solution.py:115
  80.1 15.1 %shard_map.239 = (bf16[768,384]{1,0:T(8,128)(2,1)}, bf16[1536,256]{1,0:T(8,128)(2,1)}, f32[3,8,1536]{2,1,0:T(8,128)}) custom-call(bf16[3,1536,128]{2,1,0:T(8,128)(2,1)} %get-tuple-element.136.query_ref, bf16[1536,128]{1,0:T(8,128)(2,1)} %get-tuple-element.137.key_ref, bf16[1536,128]{1,0:T(8,128)(2,1)} %get-tuple-element.138.value_ref, s32[1536,1]{1,0:T(8,128)} %copy.55.start_ref), custom_call_target="tpu_custom_call" | custom-call | flops 550000000 | bytes 1800000 | tf_op jit(solution)/shard_map/pallas_call | solution.py:175
  95.2 7.0 %collective-permute-done.1 = bf16[136,1536]{1,0:T(8,128)(2,1)S(1)} collective-permute-done((bf16[136,1536]{1,0:T(8,128)(2,1)S(1)}, bf16[136,1536]{1,0:T(8,128)(2,1)S(1)}, u32[]{:S(2)}, u32[]{:S(2)}) %collective-permute-start.1) | collective-permute-done | bytes 417824 | tf_op jit(solution)/shard_map/ppermute | solution.py:944
  107.8 12.9 %collective-permute-done.3 = bf16[1,4,48,1536]{3,2,1,0:T(8,128)(2,1)S(1)} collective-permute-done((bf16[1,4,48,1536]{3,2,1,0:T(8,128)(2,1)S(1)}, bf16[1,4,48,1536]{3,2,1,0:T(8,128)(2,1)S(1)}, u32[]{:S(2)}, u32[]{:S(2)}) %collective-permute-start.3) | collective-permute-done | bytes 589856 | tf_op jit(solution)/shard_map/ppermute | solution.py:954
  122.4 17.9 %collective-permute-done.5 = bf16[1,4,80,1536]{3,2,1,0:T(8,128)(2,1)} collective-permute-done((bf16[1,4,80,1536]{3,2,1,0:T(8,128)(2,1)S(1)}, bf16[1,4,80,1536]{3,2,1,0:T(8,128)(2,1)}, u32[]{:S(2)}, u32[]{:S(2)}) %collective-permute-start.5) | collective-permute-done | bytes 983072 | tf_op jit(solution)/shard_map/ppermute | solution.py:954
  157.9 21.6 %shard_map.240 = (bf16[5,2,4,64,1536]{4,3,2,1,0:T(8,128)(2,1)}, f32[5,2,4,64,128]{4,3,2,1,0:T(8,128)}, f32[2,4,8,192]{3,2,1,0:T(8,128)}, f32[2,4,8,192]{3,2,1,0:...) custom-call(s32[5]{0:T(128)} %stack.42.place_ref.refs_0_, ...), custom_call_target="tpu_custom_call" | custom-call | flops 550000000 | bytes 1800000 | tf_op jit(solution)/shard_map/pallas_call | solution.py:404
  179.4 23.6 %shard_map.241 = (bf16[5,512,1536]{2,1,0:T(8,128)(2,1)}, bf16[5,512,512]{2,1,0:T(8,128)(2,1)}, f32[5,512,512]{2,1,0:T(8,128)}, f32[5,512,512]{2,1,0:T(8,128)}) custom-call(bf16[5,512,1536]{2,1,0:T(8,128)(2,1)} %bitcast.73, f32[5,512,128]{2,1,0:T(8,128)} %bitcast.109, bf16[5,1536,512]{2,1,0:T(8,128)(2,1)} %refs_6_.5, bf16[5,1536,512]{2,1,0:T(8,128)(2,1)} %refs_7_.5, ...), custom_call_target="tpu_custom_call" | custom-call | flops 550000000 | bytes 1800000 | tf_op jit(solution)/shard_map/pallas_call | solution.py:495
  208.9 7.3 %shard_map.243 = bf16[5,8,64,1536]{3,2,1,0:T(8,128)(2,1)} custom-call(f32[8,8,192]{2,1,0:T(8,128)} %bitcast.105, f32[8,8,192]{2,1,0:T(8,128)} %bitcast.114, bf16[1536,1536]{1,0:T(8,128)(2,1)} %all-gather.9.cloned.1.call-done.cot_ref), custom_call_target="tpu_custom_call" | custom-call | flops 550000000 | bytes 1800000 | tf_op jit(solution)/shard_map/pallas_call | solution.py:463
  216.2 11.4 %shard_map.244 = (bf16[1,512,1536]{2,1,0:T(8,128)(2,1)}, f32[1,512,128]{2,1,0:T(8,128)}, bf16[1,3,2,384,256]{4,3,2,1,0:T(8,128)(2,1)}, bf16[1,3,2,384,256]{4,3,2...) custom-call(s32[5]{0:T(128)} %stack.42.place_ref.refs_0_, ...), custom_call_target="tpu_custom_call" | custom-call | flops 550000000 | bytes 1800000 | tf_op jit(solution)/shard_map/pallas_call | solution.py:572
  231.0 6.3 %shard_map.245 = bf16[4,192,1536]{2,1,0:T(8,128)(2,1)} custom-call(s32[5]{0:T(128)} %stack.42.place_ref.refs_0_, f32[8,8,192]{2,1,0:T(8,128)} %bitcast.106, bf16[5,8,64,1536]{3,2,1,0:T(8,128)(2,1)} %bitcast.78, bf16[4,192,1536]{2,1,0:T(8,128)(2,1)} %copy-done.13), custom_call_target="tpu_custom_call" | custom-call | flops 550000000 | bytes 1800000 | tf_op jit(solution)/shard_map/pallas_call | solution.py:634
  242.4 17.3 %shard_map.246 = (bf16[2,512,1536]{2,1,0:T(8,128)(2,1)}, f32[2,512,128]{2,1,0:T(8,128)}, bf16[2,3,2,384,256]{4,3,2,1,0:T(8,128)(2,1)}, bf16[2,3,2,384,256]{4,3,2...) custom-call(s32[5]{0:T(128)} %stack.42.place_ref.refs_0_, ...), custom_call_target="tpu_custom_call" | custom-call | flops 550000000 | bytes 1800000 | tf_op jit(solution)/shard_map/pallas_call | solution.py:572
  259.7 17.3 %shard_map.247 = (bf16[2,512,1536]{2,1,0:T(8,128)(2,1)}, f32[2,512,128]{2,1,0:T(8,128)}, bf16[2,3,2,384,256]{4,3,2,1,0:T(8,128)(2,1)}, bf16[2,3,2,384,256]{4,3,2...) custom-call(s32[5]{0:T(128)} %stack.42.place_ref.refs_0_, ...), custom_call_target="tpu_custom_call" | custom-call | flops 550000000 | bytes 1800000 | tf_op jit(solution)/shard_map/pallas_call | solution.py:572
  277.0 6.0 %shard_map.248 = bf16[4,208,1536]{2,1,0:T(8,128)(2,1)} custom-call(s32[5]{0:T(128)} %stack.42.place_ref.refs_0_, f32[8,8,192]{2,1,0:T(8,128)} %bitcast.107, bf16[1,8,64,1536]{3,2,1,0:T(8,128)(2,1)} %bitcast.88, bf16[2,8,64,1536]{3,2,1,0:T(8,128)(2,1)} %bitcast.84, bf16[2,8,64,1536]{3,2,1,0:T(8,128)(2,1)} %bitcast.86, f32[1,8,64,128]{3,2,1,0:T(8,128)} %bitcast.110, ...), custom_call_target="tpu_custom_call" | custom-call | flops 550000000 | bytes 1800000 | tf_op jit(solution)/shard_map/pallas_call | solution.py:634
  289.4 6.6 %shard_map.249 = bf16[4,208,1536]{2,1,0:T(8,128)(2,1)} custom-call(s32[5]{0:T(128)} %stack.42.place_ref.refs_0_, f32[8,8,192]{2,1,0:T(8,128)} %bitcast.108, bf16[1,8,64,1536]{3,2,1,0:T(8,128)(2,1)} %bitcast.89, bf16[2,8,64,1536]{3,2,1,0:T(8,128)(2,1)} %bitcast.85, bf16[2,8,64,1536]{3,2,1,0:T(8,128)(2,1)} %bitcast.87, f32[1,8,64,128]{3,2,1,0:T(8,128)} %bitcast.111, ...), custom_call_target="tpu_custom_call" | custom-call | flops 550000000 | bytes 1800000 | tf_op jit(solution)/shard_map/pallas_call | solution.py:634
  310.4 45.4 %collective-permute-done.15.got_a_ref = bf16[2,3,2,384,256]{4,3,2,1,0:T(8,128)(2,1)S(1)} collective-permute-done((bf16[2,3,2,384,256]{4,3,2,1,0:T(8,128)(2,1)}, bf16[2,3,2,384,256]{4,3,2,1,0:T(8,128)(2,1)S(1)}, u32[]{:S(2)}, u32[]{:S(2)}) %collective-permute-start.15) | collective-permute-done | bytes 2359328 | tf_op jit(solution)/shard_map/ppermute | solution.py:954
  362.4 7.7 %shard_map.251 = (f32[192,1536]{1,0:T(8,128)}, bf16[208,1536]{1,0:T(8,128)(2,1)}, bf16[8,192,256]{2,1,0:T(8,128)(2,1)}) custom-call(s32[5]{0:T(128)} %stack.42.place_ref.refs_0_, bf16[4,208,1536]{2,1,0:T(8,128)(2,1)} %copy-done.4, f32[64,192]{1,0:T(8,128)} %get-tuple-element.176.gates_ref, f32[192,1536]{1,0:T(8,128)} %get-tuple-element.150.middle_ref, ...), custom_call_target="tpu_custom_call" | custom-call | flops 550000000 | bytes 1800000 | tf_op jit(solution)/shard_map/pallas_call | solution.py:707
  376.1 6.7 %shard_map.252 = (bf16[3,3,384,256]{3,2,1,0:T(8,128)(2,1)}, bf16[3,3,384,256]{3,2,1,0:T(8,128)(2,1)}, bf16[3,3,384,256]{3,2,1,0:T(8,128)(2,1)}, bf16[3,3,384,256]{3,2,1,0:T(8,128)(2,1)}) custom-call(s32[5]{0:T(128)} %stack.42.place_ref.refs_0_, ...), custom_call_target="tpu_custom_call", output_to_operand_aliasing={{0}: (5, {}), {1}: (6, {}), {2}: (7, {}), {3}: (8, {})} | custom-call | flops 550000000 | bytes 1800000 | tf_op jit(solution)/shard_map/pallas_call | solution.py:869
  386.7 29.6 %all-to-all-done.2 = bf16[8,192,256]{2,1,0:T(8,128)(2,1)S(1)} async-done(((bf16[8,192,256]{2,1,0:T(8,128)(2,1)}), bf16[8,192,256]{2,1,0:T(8,128)(2,1)S(1)}, u32[]{:S(2)}, u32[]{:S(2)}) %all-to-all-start.2) | async-done | bytes 786464 | tf_op jit(solution)/shard_map/all_to_all | solution.py:1142
  417.2 27.6 %shard_map.253 = (bf16[8,208,384]{2,1,0:T(8,128)(2,1)}, bf16[1536,384]{1,0:T(8,128)(2,1)}) custom-call(bf16[3,1536,128]{2,1,0:T(8,128)(2,1)} %get-tuple-element.136.query_ref, bf16[1536,128]{1,0:T(8,128)(2,1)} %get-tuple-element.137.key_ref, bf16[1536,128]{1,0:T(8,128)(2,1)} %get-tuple-element.138.value_ref, bf16[1536,256]{1,0:T(8,128)(2,1)} %bitcast.95, ...), custom_call_target="tpu_custom_call" | custom-call | flops 550000000 | bytes 1800000 | tf_op jit(solution)/shard_map/pallas_call | solution.py:285
  449.2 8.7 %shard_map.254 = (bf16[1,1,2,384,256]{4,3,2,1,0:T(8,128)(2,1)}, bf16[1,1,2,384,256]{4,3,2,1,0:T(8,128)(2,1)}, bf16[1,1,2,384,256]{4,3,2,1,0:T(8,128)(2,1)}, bf16...) custom-call(s32[5]{0:T(128)} %stack.42.place_ref.refs_0_, bf16[1664,1536]{1,0:T(8,128)(2,1)} %all-gather.11.cloned.1.call-done.refs_1_, ...), custom_call_target="tpu_custom_call" | custom-call | flops 550000000 | bytes 1800000 | tf_op jit(solution)/shard_map/pallas_call | solution.py:835
  464.2 6.5 %shard_map.256 = (bf16[2,3,384,256]{3,2,1,0:T(8,128)(2,1)}, bf16[2,3,384,256]{3,2,1,0:T(8,128)(2,1)}, bf16[2,3,384,256]{3,2,1,0:T(8,128)(2,1)}, bf16[2,3,384,256]{3,2,1,0:T(8,128)(2,1)}) custom-call(s32[5]{0:T(128)} %stack.42.place_ref.refs_0_, bf16[2,3,2,384,256]{4,3,2,1,0:T(8,128)(2,1)} %get-tuple-element.219.keep_a_ref, ...), custom_call_target="tpu_custom_call" | custom-call | flops 550000000 | bytes 1800000 | tf_op jit(solution)/shard_map/pallas_call | solution.py:869
  482.2 8.9 %shard_map.257 = (f32[192,1536]{1,0:T(8,128)}, f32[8,384]{1,0:T(8,128)}) custom-call(s32[5]{0:T(128)} %stack.42.place_ref.refs_0_, bf16[8,208,384]{2,1,0:T(8,128)(2,1)} %copy-done.3, bf16[8,208,384]{2,1,0:T(8,128)(2,1)} %copy-done.3, bf16[2,4,80,1536]{3,2,1,0:T(8,128)(2,1)} %maximum_select_fusion.1.mine_a_ref, ...), custom_call_target="tpu_custom_call" | custom-call | flops 550000000 | bytes 1800000 | tf_op jit(solution)/shard_map/pallas_call | solution.py:766
  493.5 6.8 %shard_map.258 = (f32[5,384,512]{2,1,0:T(8,128)}, f32[5,384,512]{2,1,0:T(8,128)}, f32[5,384,512]{2,1,0:T(8,128)}) custom-call(bf16[3,3,384,256]{3,2,1,0:T(8,128)(2,1)} %get-tuple-element.228.held_a_ref, bf16[3,3,384,256]{3,2,1,0:T(8,128)(2,1)} %collective-permute-done.19.got_a_ref, bf16[3,3,384,256]{3,2,1,0:T(8,128)(2,1)} %get-tuple-element.229.held_b_ref, ...), custom_call_target="tpu_custom_call" | custom-call | flops 550000000 | bytes 1800000 | tf_op jit(solution)/shard_map/pallas_call | solution.py:894
  (190 shorter events, 141.5 us)
Async XLA Ops:
  7.2 56.9 %all-gather.5.cloned.1.call-start = ((), (), s32[]{:S(2)}) async-start(), calls=%async_computation.4 | async-start | bytes 5308416 | tf_op jit(solution)/shard_map/all_gather | solution.py:938
  8.0 149.9 %all-gather.7.cloned.1.call-start = ((), (), s32[]{:S(2)}) async-start(), calls=%async_computation.5 | async-start | bytes 5308416 | tf_op jit(solution)/shard_map/all_gather | solution.py:938
  65.0 37.3 %collective-permute-start.1 = (bf16[136,1536]{1,0:T(8,128)(2,1)S(1)}, bf16[136,1536]{1,0:T(8,128)(2,1)S(1)}, u32[]{:S(2)}, u32[]{:S(2)}) collective-permute-start(bf16[136,1536]{1,0:T(8,128)(2,1)S(1)} %fusion.2), channel_id=1, source_target_pairs={{0,2},{1,3},{2,0},{3,1},{4,6},{5,7},{6,4},{7,5},{8,10},{9,11},{10,... | collective-permute-start | bytes 1253384 | tf_op jit(solution)/shard_map/ppermute | solution.py:944
  65.5 36.7 %collective-permute-start.2 = (bf16[136,1536]{1,0:T(8,128)(2,1)S(1)}, bf16[136,1536]{1,0:T(8,128)(2,1)S(1)}, u32[]{:S(2)}, u32[]{:S(2)}) collective-permute-start(bf16[136,1536]{1,0:T(8,128)(2,1)S(1)} %fusion.2), channel_id=1, source_target_pairs={{0,1},{1,2},{2,3},{3,0},{4,5},{5,6},{6,7},{7,4},{8,9},{9,10},{10,1... | collective-permute-start | bytes 1253384 | tf_op jit(solution)/shard_map/ppermute | solution.py:944
  95.2 113.7 %all-gather.9.cloned.1.call-start = ((), (), s32[]{:S(2)}) async-start(), calls=%async_computation.6 | async-start | bytes 5308416 | tf_op jit(solution)/shard_map/all_gather | solution.py:938
  107.1 33.2 %collective-permute-start.5 = (bf16[1,4,80,1536]{3,2,1,0:T(8,128)(2,1)S(1)}, bf16[1,4,80,1536]{3,2,1,0:T(8,128)(2,1)}, u32[]{:S(2)}, u32[]{:S(2)}) collective-permute-start(bf16[1,4,80,1536]{3,2,1,0:T(8,128)(2,1)S(1)} %dynamic-slice_bitcast_fusion), channel_id=1, source_target_pairs={{0,8},{8,0},{16,24},{24,16},{1,9},{9,1},{17,25},{25,17},{2,10},{10... | collective-permute-start | bytes 2949128 | tf_op jit(solution)/shard_map/ppermute | solution.py:954
  153.4 49.6 %collective-permute-start.8 = (bf16[2,4,80,1536]{3,2,1,0:T(8,128)(2,1)}, bf16[2,4,80,1536]{3,2,1,0:T(8,128)(2,1)}, u32[]{:S(2)}, u32[]{:S(2)}) collective-permute-start(bf16[2,4,80,1536]{3,2,1,0:T(8,128)(2,1)} %maximum_select_fusion.1.mine_a_ref), channel_id=1, source_target_pairs={{0,16},{8,24},{16,0},{24,8},{1,17},{9,25},{17,1},{25,9},{2,18},{10... | collective-permute-start | bytes 5898248 | tf_op jit(solution)/shard_map/ppermute | solution.py:954
  227.6 49.4 %collective-permute-start.10 = (bf16[1,3,2,384,256]{4,3,2,1,0:T(8,128)(2,1)}, bf16[1,3,2,384,256]{4,3,2,1,0:T(8,128)(2,1)}, u32[]{:S(2)}, u32[]{:S(2)}) collective-permute-start(bf16[1,3,2,384,256]{4,3,2,1,0:T(8,128)(2,1)} %get-tuple-element.172), channel_id=1, source_target_pairs={{0,8},{8,0},{16,24},{24,16},{1,9},{9,1},{17,25},{25,17},{2,10},{10... | collective-permute-start | bytes 3538952 | tf_op jit(solution)/shard_map/ppermute | solution.py:954
  229.0 47.9 %collective-permute-start.11 = (bf16[1,3,2,384,256]{4,3,2,1,0:T(8,128)(2,1)}, bf16[1,3,2,384,256]{4,3,2,1,0:T(8,128)(2,1)}, u32[]{:S(2)}, u32[]{:S(2)}) collective-permute-start(bf16[1,3,2,384,256]{4,3,2,1,0:T(8,128)(2,1)} %get-tuple-element.173), channel_id=1, source_target_pairs={{0,16},{8,24},{16,0},{24,8},{1,17},{9,25},{17,1},{25,9},{2,18},{10... | collective-permute-start | bytes 3538952 | tf_op jit(solution)/shard_map/ppermute | solution.py:954
  237.3 58.9 %all-to-all-start = ((bf16[4,192,1536]{2,1,0:T(8,128)(2,1)}), bf16[4,192,1536]{2,1,0:T(8,128)(2,1)S(1)}, u32[]{:S(2)}, u32[]{:S(2)}) async-start(bf16[4,192,1536]{2,1,0:T(8,128)(2,1)} %shard_map.245), calls=%async_computation | async-start | bytes 4718592 | tf_op jit(solution)/shard_map/all_to_all | solution.py:1104
  297.6 63.3 %all-to-all-start.1 = ((bf16[4,208,1536]{2,1,0:T(8,128)(2,1)}), bf16[4,208,1536]{2,1,0:T(8,128)(2,1)S(1)}, u32[]{:S(2)}, u32[]{:S(2)}) async-start(bf16[4,208,1536]{2,1,0:T(8,128)(2,1)} %shard_map.249), calls=%async_computation.1 | async-start | bytes 5111808 | tf_op jit(solution)/shard_map/all_to_all | solution.py:1113
  302.6 146.6 %all-gather.11.cloned.1.call-start = ((), (), s32[]{:S(2)}) async-start(), calls=%async_computation.7 | async-start | bytes 5750784 | tf_op jit(solution)/shard_map/all_gather | solution.py:938
  302.6 53.2 %collective-permute-start.15 = (bf16[2,3,2,384,256]{4,3,2,1,0:T(8,128)(2,1)}, bf16[2,3,2,384,256]{4,3,2,1,0:T(8,128)(2,1)S(1)}, u32[]{:S(2)}, u32[]{:S(2)}) collective-permute-start(bf16[2,3,2,384,256]{4,3,2,1,0:T(8,128)(2,1)} %get-tuple-element.184), channel_id=1, source_target_pairs={{0,8},{8,0},{16,24},{24,16},{1,9},{9,1},{17,25},{25,17},{2,10},{10... | collective-permute-start | bytes 7077896 | tf_op jit(solution)/shard_map/ppermute | solution.py:954
  303.0 53.2 %collective-permute-start.16 = (bf16[2,3,2,384,256]{4,3,2,1,0:T(8,128)(2,1)}, bf16[2,3,2,384,256]{4,3,2,1,0:T(8,128)(2,1)S(1)}, u32[]{:S(2)}, u32[]{:S(2)}) collective-permute-start(bf16[2,3,2,384,256]{4,3,2,1,0:T(8,128)(2,1)} %get-tuple-element.185), channel_id=1, source_target_pairs={{0,16},{8,24},{16,0},{24,8},{1,17},{9,25},{17,1},{25,9},{2,18},{10... | collective-permute-start | bytes 7077896 | tf_op jit(solution)/shard_map/ppermute | solution.py:954
  305.0 51.2 %collective-permute-start.14 = (bf16[2,4,80,1536]{3,2,1,0:T(8,128)(2,1)}, bf16[2,4,80,1536]{3,2,1,0:T(8,128)(2,1)}, u32[]{:S(2)}, u32[]{:S(2)}) collective-permute-start(bf16[2,4,80,1536]{3,2,1,0:T(8,128)(2,1)} %collective-permute-done.8.mine_b_ref), channel_id=1, source_target_pairs={{0,4},{4,0},{1,5},{5,1},{2,6},{6,2},{3,7},{7,3},{8,12},{12,8},{9,1... | collective-permute-start | bytes 5898248 | tf_op jit(solution)/shard_map/ppermute | solution.py:1133
  305.0 51.2 %collective-permute-start.13 = (bf16[2,4,80,1536]{3,2,1,0:T(8,128)(2,1)}, bf16[2,4,80,1536]{3,2,1,0:T(8,128)(2,1)}, u32[]{:S(2)}, u32[]{:S(2)}) collective-permute-start(bf16[2,4,80,1536]{3,2,1,0:T(8,128)(2,1)} %maximum_select_fusion.1.mine_a_ref), channel_id=1, source_target_pairs={{0,4},{4,0},{1,5},{5,1},{2,6},{6,2},{3,7},{7,3},{8,12},{12,8},{9,1... | collective-permute-start | bytes 5898248 | tf_op jit(solution)/shard_map/ppermute | solution.py:1133
  370.0 94.2 %collective-permute-start.21 = (bf16[2,3,2,384,256]{4,3,2,1,0:T(8,128)(2,1)}, bf16[2,3,2,384,256]{4,3,2,1,0:T(8,128)(2,1)}, u32[]{:S(2)}, u32[]{:S(2)}) collective-permute-start(bf16[2,3,2,384,256]{4,3,2,1,0:T(8,128)(2,1)} %get-tuple-element.220), channel_id=1, source_target_pairs={{0,8},{8,0},{16,24},{24,16},{1,9},{9,1},{17,25},{25,17},{2,10},{10... | collective-permute-start | bytes 7077896 | tf_op jit(solution)/shard_map/ppermute | solution.py:954
  370.5 93.7 %collective-permute-start.22 = (bf16[2,3,2,384,256]{4,3,2,1,0:T(8,128)(2,1)}, bf16[2,3,2,384,256]{4,3,2,1,0:T(8,128)(2,1)}, u32[]{:S(2)}, u32[]{:S(2)}) collective-permute-start(bf16[2,3,2,384,256]{4,3,2,1,0:T(8,128)(2,1)} %get-tuple-element.222), channel_id=1, source_target_pairs={{0,16},{8,24},{16,0},{24,8},{1,17},{9,25},{17,1},{25,9},{2,18},{10... | collective-permute-start | bytes 7077896 | tf_op jit(solution)/shard_map/ppermute | solution.py:954
  372.5 43.8 %all-to-all-start.2 = ((bf16[8,192,256]{2,1,0:T(8,128)(2,1)}), bf16[8,192,256]{2,1,0:T(8,128)(2,1)S(1)}, u32[]{:S(2)}, u32[]{:S(2)}) async-start(bf16[8,192,256]{2,1,0:T(8,128)(2,1)} %get-tuple-element.190), calls=%async_computation.2 | async-start | bytes 1572864 | tf_op jit(solution)/shard_map/all_to_all | solution.py:1142
  382.7 78.6 %collective-permute-start.19 = (bf16[3,3,384,256]{3,2,1,0:T(8,128)(2,1)}, bf16[3,3,384,256]{3,2,1,0:T(8,128)(2,1)}, u32[]{:S(2)}, u32[]{:S(2)}) collective-permute-start(bf16[3,3,384,256]{3,2,1,0:T(8,128)(2,1)} %get-tuple-element.217), channel_id=1, source_target_pairs={{0,16},{8,24},{16,0},{24,8},{1,17},{9,25},{17,1},{25,9},{2,18},{10... | collective-permute-start | bytes 5308424 | tf_op jit(solution)/shard_map/ppermute | solution.py:954
  383.9 78.6 %collective-permute-start.20 = (bf16[3,3,384,256]{3,2,1,0:T(8,128)(2,1)}, bf16[3,3,384,256]{3,2,1,0:T(8,128)(2,1)}, u32[]{:S(2)}, u32[]{:S(2)}) collective-permute-start(bf16[3,3,384,256]{3,2,1,0:T(8,128)(2,1)} %get-tuple-element.218), channel_id=1, source_target_pairs={{0,8},{8,0},{16,24},{24,16},{1,9},{9,1},{17,25},{25,17},{2,10},{10... | collective-permute-start | bytes 5308424 | tf_op jit(solution)/shard_map/ppermute | solution.py:954
  444.8 36.4 %all-to-all-start.3 = ((bf16[8,208,384]{2,1,0:T(8,128)(2,1)}), bf16[8,208,384]{2,1,0:T(8,128)(2,1)S(1)}, u32[]{:S(2)}, u32[]{:S(2)}) async-start(bf16[8,208,384]{2,1,0:T(8,128)(2,1)} %get-tuple-element.208), calls=%async_computation.3 | async-start | bytes 2555904 | tf_op jit(solution)/shard_map/all_to_all | solution.py:1151
  470.7 42.0 %collective-permute-start.27 = (bf16[2,3,384,256]{3,2,1,0:T(8,128)(2,1)}, bf16[2,3,384,256]{3,2,1,0:T(8,128)(2,1)S(1)}, u32[]{:S(2)}, u32[]{:S(2)}) collective-permute-start(bf16[2,3,384,256]{3,2,1,0:T(8,128)(2,1)} %get-tuple-element.236), channel_id=1, source_target_pairs={{0,16},{8,24},{16,0},{24,8},{1,17},{9,25},{17,1},{25,9},{2,18},{10... | collective-permute-start | bytes 3538952 | tf_op jit(solution)/shard_map/ppermute | solution.py:954
  471.1 41.6 %collective-permute-start.28 = (bf16[2,3,384,256]{3,2,1,0:T(8,128)(2,1)}, bf16[2,3,384,256]{3,2,1,0:T(8,128)(2,1)}, u32[]{:S(2)}, u32[]{:S(2)}) collective-permute-start(bf16[2,3,384,256]{3,2,1,0:T(8,128)(2,1)} %get-tuple-element.238), channel_id=1, source_target_pairs={{0,8},{8,0},{16,24},{24,16},{1,9},{9,1},{17,25},{25,17},{2,10},{10... | collective-permute-start | bytes 3538952 | tf_op jit(solution)/shard_map/ppermute | solution.py:954
  (38 other events, 343.5 us)
Sparse Core Ops, SparseCore 0:
  9.7 54.3 all-gather.4
  95.3 51.2 all-gather.6
  153.5 52.9 all-gather.8
  370.2 69.5 all-gather.10

commit v3 on v2

--- a/solution.py
+++ b/solution.py
@@ -1074,8 +1074,8 @@
             w_out_mine = cube_step(w_out_mine, "dp", bit, n_dp)
         in_part = cube_step(in_part, "dp", 0, n_dp)
         w_out_mine = lines_first(w_out_mine)
-        w_out_other = lax.ppermute(after(w_out_mine, in_part), "row", SWAP)
         route_rows = cube_gather(route_rows, "row", n_row)[:, :, : TOP * rows].reshape(members, TOP, rows)
+        w_out_other = lax.ppermute(after(w_out_mine, in_part, route_rows), "row", SWAP)
         cot_all = gather_group(after(cotangent, w_out_other))
         x, slot_gate, rank, gate, normed_two, middle, gates = middle_and_dispatch(
             place, att_all, w_out_mine, w_out_other, tok_all, route_rows, gain_two, w_router_rows, local_experts

time: 530 us -> 528 us (level)
  waiting for transfers between devices: 183 us -> 176 us
where the time goes in v3:
time: 528 us; the launch traced here: 523 us
  Pallas kernels  234 us (44%)
  waiting for transfers between devices  176 us (33%)
  starting transfers between devices  52.5 us (10%)
  local copies, waits for them, and re-layouts  32.7 us (6%)
  between operations  14.5 us (3%)
  other arithmetic  13.3 us (3%)
    ppermute x23, waiting for transfers between devices, flip(): return lax.ppermute(value, axis, [(i, i ^ 1 << bit) for i in range(size)])  86.6 us
    pallas_call x3, Pallas kernels, run_experts_back(): call(lambda *refs: expert_back_kernel(*refs, fast=fast), (count,), 1, [ta...  46 us
    all_gather x4, waiting for transfers between devices, gather_group(): return lax.all_gather(block, ('row', 'col'), axis=0, tiled=True)  43 us
    ppermute x23, starting transfers between devices, flip(): return lax.ppermute(value, axis, [(i, i ^ 1 << bit) for i in range(size)])  28.8 us
    pallas_call x1, Pallas kernels, attend_back(): call(attend_back_kernel, (total // QUERY_BLOCK,), 0, [whole(item.shape) f...  27.6 us
    all_to_all x1, waiting for transfers between devices, local(): lax.all_to_all(attended_grad, ('row', 'col'), 0, 0, tiled=True)  26.3 us
    pallas_call x4, Pallas kernels, combine(): call(lambda *refs: combine_kernel(*refs, pieces=len(parts), with_dots=boo...  24.7 us
    pallas_call x1, Pallas kernels, run_experts(): call(expert_kernel, (count,), 0, [per_expert(slots, width), per_expert(sl...  23.6 us
  transfers between devices with their start and end apart: 39, of which 18 were waited for; matrix products, arithmetic and copies ran while one was open for 6% of the time, Pallas kernels for 43%

profile of v3, /device:TPU:0, one launch (start us, length us, event | category | flops | bytes accessed | tf_op | source)
XLA Modules:
  0.0 522.9 jit_solution(5287482082976669183)
XLA Ops:
  21.9 42.3 %all-gather.5.cloned.1.call-done.tok_ref.tok_a_ref.tok_b_ref = bf16[1536,1536]{1,0:T(8,128)(2,1)} async-done(((bf16[192,1536]{1,0:T(8,128)(2,1)}), bf16[1536,1536]{1,0:T(8,128)(2,1)}) %all-gather.5.cloned.1.call-update) | async-done | bytes 4718608 | tf_op jit(solution)/shard_map/all_gather | solution.py:938
  70.9 9.2 %shard_map.238 = (bf16[3,1536,128]{2,1,0:T(8,128)(2,1)}, bf16[1536,128]{1,0:T(8,128)(2,1)}, bf16[1536,128]{1,0:T(8,128)(2,1)}, bf16[1536,1536]{1,0:T(8,128)(2,1)}) custom-call(bf16[1536,1536]{1,0:T(8,128)(2,1)} %all-gather.5.cloned.1.call-done.tok_ref.tok_a_ref.tok_b_ref, f32[1,1536]{1,0:T(1,128)} %broadcast_in_dim.46.gain_ref, ...), custom_call_target="tpu_custom_call" | custom-call | flops 550000000 | bytes 1800000 | tf_op jit(solution)/shard_map/pallas_call | solution.py:115
  80.1 15.1 %shard_map.239 = (bf16[768,384]{1,0:T(8,128)(2,1)}, bf16[1536,256]{1,0:T(8,128)(2,1)}, f32[3,8,1536]{2,1,0:T(8,128)}) custom-call(bf16[3,1536,128]{2,1,0:T(8,128)(2,1)} %get-tuple-element.136.query_ref, bf16[1536,128]{1,0:T(8,128)(2,1)} %get-tuple-element.137.key_ref, bf16[1536,128]{1,0:T(8,128)(2,1)} %get-tuple-element.138.value_ref, s32[1536,1]{1,0:T(8,128)} %copy.55.start_ref), custom_call_target="tpu_custom_call" | custom-call | flops 550000000 | bytes 1800000 | tf_op jit(solution)/shard_map/pallas_call | solution.py:175
  95.8 6.4 %collective-permute-done.1 = bf16[136,1536]{1,0:T(8,128)(2,1)S(1)} collective-permute-done((bf16[136,1536]{1,0:T(8,128)(2,1)S(1)}, bf16[136,1536]{1,0:T(8,128)(2,1)S(1)}, u32[]{:S(2)}, u32[]{:S(2)}) %collective-permute-start.1) | collective-permute-done | bytes 417824 | tf_op jit(solution)/shard_map/ppermute | solution.py:944
  107.8 12.9 %collective-permute-done.3 = bf16[1,4,48,1536]{3,2,1,0:T(8,128)(2,1)S(1)} collective-permute-done((bf16[1,4,48,1536]{3,2,1,0:T(8,128)(2,1)S(1)}, bf16[1,4,48,1536]{3,2,1,0:T(8,128)(2,1)S(1)}, u32[]{:S(2)}, u32[]{:S(2)}) %collective-permute-start.3) | collective-permute-done | bytes 589856 | tf_op jit(solution)/shard_map/ppermute | solution.py:954
  125.3 15.0 %collective-permute-done.5 = bf16[1,4,80,1536]{3,2,1,0:T(8,128)(2,1)} collective-permute-done((bf16[1,4,80,1536]{3,2,1,0:T(8,128)(2,1)S(1)}, bf16[1,4,80,1536]{3,2,1,0:T(8,128)(2,1)}, u32[]{:S(2)}, u32[]{:S(2)}) %collective-permute-start.5) | collective-permute-done | bytes 983072 | tf_op jit(solution)/shard_map/ppermute | solution.py:954
  154.4 21.4 %shard_map.240 = (bf16[5,2,4,64,1536]{4,3,2,1,0:T(8,128)(2,1)}, f32[5,2,4,64,128]{4,3,2,1,0:T(8,128)}, f32[2,4,8,192]{3,2,1,0:T(8,128)}, f32[2,4,8,192]{3,2,1,0:...) custom-call(s32[5]{0:T(128)} %stack.42.place_ref.refs_0_, ...), custom_call_target="tpu_custom_call" | custom-call | flops 550000000 | bytes 1800000 | tf_op jit(solution)/shard_map/pallas_call | solution.py:404
  175.8 23.6 %shard_map.241 = (bf16[5,512,1536]{2,1,0:T(8,128)(2,1)}, bf16[5,512,512]{2,1,0:T(8,128)(2,1)}, f32[5,512,512]{2,1,0:T(8,128)}, f32[5,512,512]{2,1,0:T(8,128)}) custom-call(bf16[5,512,1536]{2,1,0:T(8,128)(2,1)} %bitcast.73, f32[5,512,128]{2,1,0:T(8,128)} %bitcast.109, bf16[5,1536,512]{2,1,0:T(8,128)(2,1)} %refs_6_.5, bf16[5,1536,512]{2,1,0:T(8,128)(2,1)} %refs_7_.5, ...), custom_call_target="tpu_custom_call" | custom-call | flops 550000000 | bytes 1800000 | tf_op jit(solution)/shard_map/pallas_call | solution.py:495
  205.9 7.3 %shard_map.243 = bf16[5,8,64,1536]{3,2,1,0:T(8,128)(2,1)} custom-call(f32[8,8,192]{2,1,0:T(8,128)} %bitcast.105, f32[8,8,192]{2,1,0:T(8,128)} %bitcast.114, bf16[1536,1536]{1,0:T(8,128)(2,1)} %all-gather.9.cloned.1.call-done.cot_ref), custom_call_target="tpu_custom_call" | custom-call | flops 550000000 | bytes 1800000 | tf_op jit(solution)/shard_map/pallas_call | solution.py:463
  213.2 11.4 %shard_map.244 = (bf16[1,512,1536]{2,1,0:T(8,128)(2,1)}, f32[1,512,128]{2,1,0:T(8,128)}, bf16[1,3,2,384,256]{4,3,2,1,0:T(8,128)(2,1)}, bf16[1,3,2,384,256]{4,3,2...) custom-call(s32[5]{0:T(128)} %stack.42.place_ref.refs_0_, ...), custom_call_target="tpu_custom_call" | custom-call | flops 550000000 | bytes 1800000 | tf_op jit(solution)/shard_map/pallas_call | solution.py:572
  231.8 6.3 %shard_map.245 = bf16[4,192,1536]{2,1,0:T(8,128)(2,1)} custom-call(s32[5]{0:T(128)} %stack.42.place_ref.refs_0_, f32[8,8,192]{2,1,0:T(8,128)} %bitcast.106, bf16[5,8,64,1536]{3,2,1,0:T(8,128)(2,1)} %bitcast.78, bf16[4,192,1536]{2,1,0:T(8,128)(2,1)} %copy-done.13), custom_call_target="tpu_custom_call" | custom-call | flops 550000000 | bytes 1800000 | tf_op jit(solution)/shard_map/pallas_call | solution.py:634
  241.9 17.3 %shard_map.246 = (bf16[2,512,1536]{2,1,0:T(8,128)(2,1)}, f32[2,512,128]{2,1,0:T(8,128)}, bf16[2,3,2,384,256]{4,3,2,1,0:T(8,128)(2,1)}, bf16[2,3,2,384,256]{4,3,2...) custom-call(s32[5]{0:T(128)} %stack.42.place_ref.refs_0_, ...), custom_call_target="tpu_custom_call" | custom-call | flops 550000000 | bytes 1800000 | tf_op jit(solution)/shard_map/pallas_call | solution.py:572
  259.2 17.3 %shard_map.247 = (bf16[2,512,1536]{2,1,0:T(8,128)(2,1)}, f32[2,512,128]{2,1,0:T(8,128)}, bf16[2,3,2,384,256]{4,3,2,1,0:T(8,128)(2,1)}, bf16[2,3,2,384,256]{4,3,2...) custom-call(s32[5]{0:T(128)} %stack.42.place_ref.refs_0_, ...), custom_call_target="tpu_custom_call" | custom-call | flops 550000000 | bytes 1800000 | tf_op jit(solution)/shard_map/pallas_call | solution.py:572
  289.0 6.6 %shard_map.249 = bf16[4,208,1536]{2,1,0:T(8,128)(2,1)} custom-call(s32[5]{0:T(128)} %stack.42.place_ref.refs_0_, f32[8,8,192]{2,1,0:T(8,128)} %bitcast.108, bf16[1,8,64,1536]{3,2,1,0:T(8,128)(2,1)} %bitcast.89, bf16[2,8,64,1536]{3,2,1,0:T(8,128)(2,1)} %bitcast.85, bf16[2,8,64,1536]{3,2,1,0:T(8,128)(2,1)} %bitcast.87, f32[1,8,64,128]{3,2,1,0:T(8,128)} %bitcast.111, ...), custom_call_target="tpu_custom_call" | custom-call | flops 550000000 | bytes 1800000 | tf_op jit(solution)/shard_map/pallas_call | solution.py:634
  308.2 47.1 %collective-permute-done.15.got_a_ref = bf16[2,3,2,384,256]{4,3,2,1,0:T(8,128)(2,1)S(1)} collective-permute-done((bf16[2,3,2,384,256]{4,3,2,1,0:T(8,128)(2,1)}, bf16[2,3,2,384,256]{4,3,2,1,0:T(8,128)(2,1)S(1)}, u32[]{:S(2)}, u32[]{:S(2)}) %collective-permute-start.15) | collective-permute-done | bytes 2359328 | tf_op jit(solution)/shard_map/ppermute | solution.py:954
  361.9 7.7 %shard_map.251 = (f32[192,1536]{1,0:T(8,128)}, bf16[208,1536]{1,0:T(8,128)(2,1)}, bf16[8,192,256]{2,1,0:T(8,128)(2,1)}) custom-call(s32[5]{0:T(128)} %stack.42.place_ref.refs_0_, bf16[4,208,1536]{2,1,0:T(8,128)(2,1)} %copy-done.4, f32[64,192]{1,0:T(8,128)} %get-tuple-element.176.gates_ref, f32[192,1536]{1,0:T(8,128)} %get-tuple-element.150.middle_ref, ...), custom_call_target="tpu_custom_call" | custom-call | flops 550000000 | bytes 1800000 | tf_op jit(solution)/shard_map/pallas_call | solution.py:707
  373.8 6.7 %shard_map.252 = (bf16[3,3,384,256]{3,2,1,0:T(8,128)(2,1)}, bf16[3,3,384,256]{3,2,1,0:T(8,128)(2,1)}, bf16[3,3,384,256]{3,2,1,0:T(8,128)(2,1)}, bf16[3,3,384,256]{3,2,1,0:T(8,128)(2,1)}) custom-call(s32[5]{0:T(128)} %stack.42.place_ref.refs_0_, ...), custom_call_target="tpu_custom_call", output_to_operand_aliasing={{0}: (5, {}), {1}: (6, {}), {2}: (7, {}), {3}: (8, {})} | custom-call | flops 550000000 | bytes 1800000 | tf_op jit(solution)/shard_map/pallas_call | solution.py:869
  385.2 26.3 %all-to-all-done.2 = bf16[8,192,256]{2,1,0:T(8,128)(2,1)S(1)} async-done(((bf16[8,192,256]{2,1,0:T(8,128)(2,1)}), bf16[8,192,256]{2,1,0:T(8,128)(2,1)S(1)}, u32[]{:S(2)}, u32[]{:S(2)}) %all-to-all-start.2) | async-done | bytes 786464 | tf_op jit(solution)/shard_map/all_to_all | solution.py:1142
  412.4 27.6 %shard_map.253 = (bf16[8,208,384]{2,1,0:T(8,128)(2,1)}, bf16[1536,384]{1,0:T(8,128)(2,1)}) custom-call(bf16[3,1536,128]{2,1,0:T(8,128)(2,1)} %get-tuple-element.136.query_ref, bf16[1536,128]{1,0:T(8,128)(2,1)} %get-tuple-element.137.key_ref, bf16[1536,128]{1,0:T(8,128)(2,1)} %get-tuple-element.138.value_ref, bf16[1536,256]{1,0:T(8,128)(2,1)} %bitcast.95, ...), custom_call_target="tpu_custom_call" | custom-call | flops 550000000 | bytes 1800000 | tf_op jit(solution)/shard_map/pallas_call | solution.py:285
  440.0 6.9 %all-to-all-start.3 = ((bf16[8,208,384]{2,1,0:T(8,128)(2,1)}), bf16[8,208,384]{2,1,0:T(8,128)(2,1)S(1)}, u32[]{:S(2)}, u32[]{:S(2)}) async-start(bf16[8,208,384]{2,1,0:T(8,128)(2,1)} %get-tuple-element.208), calls=%async_computation.3 | async-start | bytes 2555904 | tf_op jit(solution)/shard_map/all_to_all | solution.py:1151
  446.9 8.7 %shard_map.254 = (bf16[1,1,2,384,256]{4,3,2,1,0:T(8,128)(2,1)}, bf16[1,1,2,384,256]{4,3,2,1,0:T(8,128)(2,1)}, bf16[1,1,2,384,256]{4,3,2,1,0:T(8,128)(2,1)}, bf16...) custom-call(s32[5]{0:T(128)} %stack.42.place_ref.refs_0_, bf16[1664,1536]{1,0:T(8,128)(2,1)} %all-gather.11.cloned.1.call-done.refs_1_, ...), custom_call_target="tpu_custom_call" | custom-call | flops 550000000 | bytes 1800000 | tf_op jit(solution)/shard_map/pallas_call | solution.py:835
  462.2 6.5 %shard_map.256 = (bf16[2,3,384,256]{3,2,1,0:T(8,128)(2,1)}, bf16[2,3,384,256]{3,2,1,0:T(8,128)(2,1)}, bf16[2,3,384,256]{3,2,1,0:T(8,128)(2,1)}, bf16[2,3,384,256]{3,2,1,0:T(8,128)(2,1)}) custom-call(s32[5]{0:T(128)} %stack.42.place_ref.refs_0_, bf16[2,3,2,384,256]{4,3,2,1,0:T(8,128)(2,1)} %get-tuple-element.219.keep_a_ref, ...), custom_call_target="tpu_custom_call" | custom-call | flops 550000000 | bytes 1800000 | tf_op jit(solution)/shard_map/pallas_call | solution.py:869
  482.0 8.9 %shard_map.257 = (f32[192,1536]{1,0:T(8,128)}, f32[8,384]{1,0:T(8,128)}) custom-call(s32[5]{0:T(128)} %stack.42.place_ref.refs_0_, bf16[8,208,384]{2,1,0:T(8,128)(2,1)} %copy-done.3, bf16[8,208,384]{2,1,0:T(8,128)(2,1)} %copy-done.3, bf16[2,4,80,1536]{3,2,1,0:T(8,128)(2,1)} %maximum_select_fusion.1.mine_a_ref, ...), custom_call_target="tpu_custom_call" | custom-call | flops 550000000 | bytes 1800000 | tf_op jit(solution)/shard_map/pallas_call | solution.py:766
  493.1 6.8 %shard_map.258 = (f32[5,384,512]{2,1,0:T(8,128)}, f32[5,384,512]{2,1,0:T(8,128)}, f32[5,384,512]{2,1,0:T(8,128)}) custom-call(bf16[3,3,384,256]{3,2,1,0:T(8,128)(2,1)} %get-tuple-element.228.held_a_ref, bf16[3,3,384,256]{3,2,1,0:T(8,128)(2,1)} %collective-permute-done.19.got_a_ref, bf16[3,3,384,256]{3,2,1,0:T(8,128)(2,1)} %get-tuple-element.229.held_b_ref, ...), custom_call_target="tpu_custom_call" | custom-call | flops 550000000 | bytes 1800000 | tf_op jit(solution)/shard_map/pallas_call | solution.py:894
  (190 shorter events, 143.4 us)
Async XLA Ops:
  7.2 56.9 %all-gather.5.cloned.1.call-start = ((), (), s32[]{:S(2)}) async-start(), calls=%async_computation.4 | async-start | bytes 5308416 | tf_op jit(solution)/shard_map/all_gather | solution.py:938
  8.0 146.4 %all-gather.7.cloned.1.call-start = ((), (), s32[]{:S(2)}) async-start(), calls=%async_computation.5 | async-start | bytes 5308416 | tf_op jit(solution)/shard_map/all_gather | solution.py:938
  65.0 37.3 %collective-permute-start.1 = (bf16[136,1536]{1,0:T(8,128)(2,1)S(1)}, bf16[136,1536]{1,0:T(8,128)(2,1)S(1)}, u32[]{:S(2)}, u32[]{:S(2)}) collective-permute-start(bf16[136,1536]{1,0:T(8,128)(2,1)S(1)} %fusion.2), channel_id=1, source_target_pairs={{0,2},{1,3},{2,0},{3,1},{4,6},{5,7},{6,4},{7,5},{8,10},{9,11},{10,... | collective-permute-start | bytes 1253384 | tf_op jit(solution)/shard_map/ppermute | solution.py:944
  65.5 36.7 %collective-permute-start.2 = (bf16[136,1536]{1,0:T(8,128)(2,1)S(1)}, bf16[136,1536]{1,0:T(8,128)(2,1)S(1)}, u32[]{:S(2)}, u32[]{:S(2)}) collective-permute-start(bf16[136,1536]{1,0:T(8,128)(2,1)S(1)} %fusion.2), channel_id=1, source_target_pairs={{0,1},{1,2},{2,3},{3,0},{4,5},{5,6},{6,7},{7,4},{8,9},{9,10},{10,1... | collective-permute-start | bytes 1253384 | tf_op jit(solution)/shard_map/ppermute | solution.py:944
  95.2 110.7 %all-gather.9.cloned.1.call-start = ((), (), s32[]{:S(2)}) async-start(), calls=%async_computation.6 | async-start | bytes 5308416 | tf_op jit(solution)/shard_map/all_gather | solution.py:938
  107.1 33.2 %collective-permute-start.5 = (bf16[1,4,80,1536]{3,2,1,0:T(8,128)(2,1)S(1)}, bf16[1,4,80,1536]{3,2,1,0:T(8,128)(2,1)}, u32[]{:S(2)}, u32[]{:S(2)}) collective-permute-start(bf16[1,4,80,1536]{3,2,1,0:T(8,128)(2,1)S(1)} %dynamic-slice_bitcast_fusion), channel_id=1, source_target_pairs={{0,8},{8,0},{16,24},{24,16},{1,9},{9,1},{17,25},{25,17},{2,10},{10... | collective-permute-start | bytes 2949128 | tf_op jit(solution)/shard_map/ppermute | solution.py:954
  152.8 46.6 %collective-permute-start.8 = (bf16[2,4,80,1536]{3,2,1,0:T(8,128)(2,1)}, bf16[2,4,80,1536]{3,2,1,0:T(8,128)(2,1)}, u32[]{:S(2)}, u32[]{:S(2)}) collective-permute-start(bf16[2,4,80,1536]{3,2,1,0:T(8,128)(2,1)} %maximum_select_fusion.1.mine_a_ref), channel_id=1, source_target_pairs={{0,16},{8,24},{16,0},{24,8},{1,17},{9,25},{17,1},{25,9},{2,18},{10... | collective-permute-start | bytes 5898248 | tf_op jit(solution)/shard_map/ppermute | solution.py:954
  224.6 51.9 %collective-permute-start.10 = (bf16[1,3,2,384,256]{4,3,2,1,0:T(8,128)(2,1)}, bf16[1,3,2,384,256]{4,3,2,1,0:T(8,128)(2,1)}, u32[]{:S(2)}, u32[]{:S(2)}) collective-permute-start(bf16[1,3,2,384,256]{4,3,2,1,0:T(8,128)(2,1)} %get-tuple-element.172), channel_id=1, source_target_pairs={{0,8},{8,0},{16,24},{24,16},{1,9},{9,1},{17,25},{25,17},{2,10},{10... | collective-permute-start | bytes 3538952 | tf_op jit(solution)/shard_map/ppermute | solution.py:954
  226.1 50.4 %collective-permute-start.11 = (bf16[1,3,2,384,256]{4,3,2,1,0:T(8,128)(2,1)}, bf16[1,3,2,384,256]{4,3,2,1,0:T(8,128)(2,1)}, u32[]{:S(2)}, u32[]{:S(2)}) collective-permute-start(bf16[1,3,2,384,256]{4,3,2,1,0:T(8,128)(2,1)} %get-tuple-element.173), channel_id=1, source_target_pairs={{0,16},{8,24},{16,0},{24,8},{1,17},{9,25},{17,1},{25,9},{2,18},{10... | collective-permute-start | bytes 3538952 | tf_op jit(solution)/shard_map/ppermute | solution.py:954
  238.1 57.7 %all-to-all-start = ((bf16[4,192,1536]{2,1,0:T(8,128)(2,1)}), bf16[4,192,1536]{2,1,0:T(8,128)(2,1)S(1)}, u32[]{:S(2)}, u32[]{:S(2)}) async-start(bf16[4,192,1536]{2,1,0:T(8,128)(2,1)} %shard_map.245), calls=%async_computation | async-start | bytes 4718592 | tf_op jit(solution)/shard_map/all_to_all | solution.py:1104
  297.3 63.1 %all-to-all-start.1 = ((bf16[4,208,1536]{2,1,0:T(8,128)(2,1)}), bf16[4,208,1536]{2,1,0:T(8,128)(2,1)S(1)}, u32[]{:S(2)}, u32[]{:S(2)}) async-start(bf16[4,208,1536]{2,1,0:T(8,128)(2,1)} %shard_map.249), calls=%async_computation.1 | async-start | bytes 5111808 | tf_op jit(solution)/shard_map/all_to_all | solution.py:1113
  302.1 144.8 %all-gather.11.cloned.1.call-start = ((), (), s32[]{:S(2)}) async-start(), calls=%async_computation.7 | async-start | bytes 5750784 | tf_op jit(solution)/shard_map/all_gather | solution.py:938
  302.1 53.2 %collective-permute-start.15 = (bf16[2,3,2,384,256]{4,3,2,1,0:T(8,128)(2,1)}, bf16[2,3,2,384,256]{4,3,2,1,0:T(8,128)(2,1)S(1)}, u32[]{:S(2)}, u32[]{:S(2)}) collective-permute-start(bf16[2,3,2,384,256]{4,3,2,1,0:T(8,128)(2,1)} %get-tuple-element.184), channel_id=1, source_target_pairs={{0,8},{8,0},{16,24},{24,16},{1,9},{9,1},{17,25},{25,17},{2,10},{10... | collective-permute-start | bytes 7077896 | tf_op jit(solution)/shard_map/ppermute | solution.py:954
  302.7 52.9 %collective-permute-start.16 = (bf16[2,3,2,384,256]{4,3,2,1,0:T(8,128)(2,1)}, bf16[2,3,2,384,256]{4,3,2,1,0:T(8,128)(2,1)S(1)}, u32[]{:S(2)}, u32[]{:S(2)}) collective-permute-start(bf16[2,3,2,384,256]{4,3,2,1,0:T(8,128)(2,1)} %get-tuple-element.185), channel_id=1, source_target_pairs={{0,16},{8,24},{16,0},{24,8},{1,17},{9,25},{17,1},{25,9},{2,18},{10... | collective-permute-start | bytes 7077896 | tf_op jit(solution)/shard_map/ppermute | solution.py:954
  302.7 52.9 %collective-permute-start.14 = (bf16[2,4,80,1536]{3,2,1,0:T(8,128)(2,1)}, bf16[2,4,80,1536]{3,2,1,0:T(8,128)(2,1)}, u32[]{:S(2)}, u32[]{:S(2)}) collective-permute-start(bf16[2,4,80,1536]{3,2,1,0:T(8,128)(2,1)} %collective-permute-done.8.mine_b_ref), channel_id=1, source_target_pairs={{0,4},{4,0},{1,5},{5,1},{2,6},{6,2},{3,7},{7,3},{8,12},{12,8},{9,1... | collective-permute-start | bytes 5898248 | tf_op jit(solution)/shard_map/ppermute | solution.py:1133
  302.7 52.9 %collective-permute-start.13 = (bf16[2,4,80,1536]{3,2,1,0:T(8,128)(2,1)}, bf16[2,4,80,1536]{3,2,1,0:T(8,128)(2,1)}, u32[]{:S(2)}, u32[]{:S(2)}) collective-permute-start(bf16[2,4,80,1536]{3,2,1,0:T(8,128)(2,1)} %maximum_select_fusion.1.mine_a_ref), channel_id=1, source_target_pairs={{0,4},{4,0},{1,5},{5,1},{2,6},{6,2},{3,7},{7,3},{8,12},{12,8},{9,1... | collective-permute-start | bytes 5898248 | tf_op jit(solution)/shard_map/ppermute | solution.py:1133
  369.6 92.6 %collective-permute-start.21 = (bf16[2,3,2,384,256]{4,3,2,1,0:T(8,128)(2,1)}, bf16[2,3,2,384,256]{4,3,2,1,0:T(8,128)(2,1)}, u32[]{:S(2)}, u32[]{:S(2)}) collective-permute-start(bf16[2,3,2,384,256]{4,3,2,1,0:T(8,128)(2,1)} %get-tuple-element.220), channel_id=1, source_target_pairs={{0,8},{8,0},{16,24},{24,16},{1,9},{9,1},{17,25},{25,17},{2,10},{10... | collective-permute-start | bytes 7077896 | tf_op jit(solution)/shard_map/ppermute | solution.py:954
  370.3 91.9 %collective-permute-start.22 = (bf16[2,3,2,384,256]{4,3,2,1,0:T(8,128)(2,1)}, bf16[2,3,2,384,256]{4,3,2,1,0:T(8,128)(2,1)}, u32[]{:S(2)}, u32[]{:S(2)}) collective-permute-start(bf16[2,3,2,384,256]{4,3,2,1,0:T(8,128)(2,1)} %get-tuple-element.222), channel_id=1, source_target_pairs={{0,16},{8,24},{16,0},{24,8},{1,17},{9,25},{17,1},{25,9},{2,18},{10... | collective-permute-start | bytes 7077896 | tf_op jit(solution)/shard_map/ppermute | solution.py:954
  370.3 41.3 %all-to-all-start.2 = ((bf16[8,192,256]{2,1,0:T(8,128)(2,1)}), bf16[8,192,256]{2,1,0:T(8,128)(2,1)S(1)}, u32[]{:S(2)}, u32[]{:S(2)}) async-start(bf16[8,192,256]{2,1,0:T(8,128)(2,1)} %get-tuple-element.190), calls=%async_computation.2 | async-start | bytes 1572864 | tf_op jit(solution)/shard_map/all_to_all | solution.py:1142
  380.5 79.9 %collective-permute-start.19 = (bf16[3,3,384,256]{3,2,1,0:T(8,128)(2,1)}, bf16[3,3,384,256]{3,2,1,0:T(8,128)(2,1)}, u32[]{:S(2)}, u32[]{:S(2)}) collective-permute-start(bf16[3,3,384,256]{3,2,1,0:T(8,128)(2,1)} %get-tuple-element.217), channel_id=1, source_target_pairs={{0,16},{8,24},{16,0},{24,8},{1,17},{9,25},{17,1},{25,9},{2,18},{10... | collective-permute-start | bytes 5308424 | tf_op jit(solution)/shard_map/ppermute | solution.py:954
  382.6 79.3 %collective-permute-start.20 = (bf16[3,3,384,256]{3,2,1,0:T(8,128)(2,1)}, bf16[3,3,384,256]{3,2,1,0:T(8,128)(2,1)}, u32[]{:S(2)}, u32[]{:S(2)}) collective-permute-start(bf16[3,3,384,256]{3,2,1,0:T(8,128)(2,1)} %get-tuple-element.218), channel_id=1, source_target_pairs={{0,8},{8,0},{16,24},{24,16},{1,9},{9,1},{17,25},{25,17},{2,10},{10... | collective-permute-start | bytes 5308424 | tf_op jit(solution)/shard_map/ppermute | solution.py:954
  440.0 41.0 %all-to-all-start.3 = ((bf16[8,208,384]{2,1,0:T(8,128)(2,1)}), bf16[8,208,384]{2,1,0:T(8,128)(2,1)S(1)}, u32[]{:S(2)}, u32[]{:S(2)}) async-start(bf16[8,208,384]{2,1,0:T(8,128)(2,1)} %get-tuple-element.208), calls=%async_computation.3 | async-start | bytes 2555904 | tf_op jit(solution)/shard_map/all_to_all | solution.py:1151
  468.6 41.8 %collective-permute-start.27 = (bf16[2,3,384,256]{3,2,1,0:T(8,128)(2,1)}, bf16[2,3,384,256]{3,2,1,0:T(8,128)(2,1)S(1)}, u32[]{:S(2)}, u32[]{:S(2)}) collective-permute-start(bf16[2,3,384,256]{3,2,1,0:T(8,128)(2,1)} %get-tuple-element.236), channel_id=1, source_target_pairs={{0,16},{8,24},{16,0},{24,8},{1,17},{9,25},{17,1},{25,9},{2,18},{10... | collective-permute-start | bytes 3538952 | tf_op jit(solution)/shard_map/ppermute | solution.py:954
  470.4 40.0 %collective-permute-start.28 = (bf16[2,3,384,256]{3,2,1,0:T(8,128)(2,1)}, bf16[2,3,384,256]{3,2,1,0:T(8,128)(2,1)}, u32[]{:S(2)}, u32[]{:S(2)}) collective-permute-start(bf16[2,3,384,256]{3,2,1,0:T(8,128)(2,1)} %get-tuple-element.238), channel_id=1, source_target_pairs={{0,8},{8,0},{16,24},{24,16},{1,9},{9,1},{17,25},{25,17},{2,10},{10... | collective-permute-start | bytes 3538952 | tf_op jit(solution)/shard_map/ppermute | solution.py:954
  (38 other events, 341.5 us)
Sparse Core Ops, SparseCore 0:
  9.7 54.3 all-gather.4
  95.3 51.2 all-gather.6
  153.0 52.9 all-gather.8
  369.7 67.7 all-gather.10
